TPU v7x, 32 devices: a whole 2x2x4 slice. The times are simulated.
32 devices in a mesh: pts: 8 (over y, x, core), lmk: 4 (over z).
Axes of the slice: x: 2, y: 2, z: 4, core: 2. Of those that a mesh axis runs over, the one named last changes fastest.
Arguments:
- points: bfloat16 [2048, 768], P('pts'), may hold values from -6 to 6
- landmarks: bfloat16 [384, 768], P('lmk'), may hold values from -6 to 6
- panels: bfloat16 [8, 384, 2048], P('pts', None, 'lmk'), may hold values from -0.3125 to 0.3125
- panel_index: int32 [1], replicated, may hold values from 0 to 7
- assignment: int32 [2048], P('pts'), may hold values from 0 to 4095, as said below
Outputs:
- centroid_sums: float32 [4096, 2048], P('pts', 'lmk')
- cluster_counts: int32 [4096], P('pts')
Inputs may be any that keep to these rules, and one draw needn't show every extreme that they name: `assignment`: owner of a cluster c is c // 512. In each aligned block of 256 points (the points of one device) at most 64 points have clusters of one owner; one owner, the same for every block, has exactly 64 points in every block.
All inputs are finite; a program needn't handle non-finite values.
Results may differ from a plain program's by a relative error of at most 0.0017.
Values may be sent and summed in bfloat16 or wider, within the bound.
No kernel may reach another device: no remote copies, remote signals or barrier semaphores. Data moves between devices by JAX's collectives and lax.ppermute only.
A program may use at most 64 MiB of HBM per device.

v0:
```python
import math

import jax
import jax.numpy as jnp
from jax import lax
from jax.experimental import pallas as pl
from jax.experimental.pallas import tpu as pltpu
from jax.sharding import PartitionSpec as P

CLUSTERS = 4096
LANES = 128
VMEM_LIMIT = 48 * 1024 * 1024
NT = (((1,), (1,)), ((), ()))


def unit_rows(values_in):
    widened = values_in.astype(jnp.float32)
    scale = lax.rsqrt(jnp.mean(widened * widened, axis=1, keepdims=True) + 1e-06)
    return (widened * scale).astype(jnp.bfloat16)


def place_kernel(groups, capacity, parts, place_ref, points_ref, assignment_ref, panel_ref, *outs):
    points_out, tags_out, mine_out, other_out = outs
    point_rows = points_ref.shape[0]
    ids = assignment_ref[...]
    owned = CLUSTERS // groups
    owners = lax.div(ids, owned)
    tags = ids - owners * owned + 1
    hits = lax.broadcasted_iota(jnp.int32, (groups, point_rows), 0) == owners
    earlier = lax.broadcasted_iota(jnp.int32, (point_rows, point_rows), 0) < lax.broadcasted_iota(
        jnp.int32, (point_rows, point_rows), 1
    )
    before = jnp.dot(
        hits.astype(jnp.float32).astype(jnp.bfloat16),
        earlier.astype(jnp.float32).astype(jnp.bfloat16),
        preferred_element_type=jnp.float32,
    )
    rank = jnp.sum(jnp.where(hits, before, 0.0), axis=0, keepdims=True).astype(jnp.int32)
    slots = owners * capacity + rank
    placed = (
        (lax.broadcasted_iota(jnp.int32, (groups * capacity, point_rows), 0) == slots)
        .astype(jnp.float32)
        .astype(jnp.bfloat16)
    )
    points_out[...] = jnp.dot(
        placed, unit_rows(points_ref[...]), preferred_element_type=jnp.float32
    ).astype(jnp.bfloat16)
    high = lax.div(tags, 256)
    which = lax.broadcasted_iota(jnp.int32, (tags_out.shape[1], point_rows), 0)
    coded = jnp.where(which == 0, high, jnp.where(which == 1, tags - high * 256, 0))
    tags_out[...] = lax.dot_general(
        placed,
        coded.astype(jnp.float32).astype(jnp.bfloat16),
        NT,
        preferred_element_type=jnp.float32,
    ).astype(jnp.bfloat16)
    half = panel_ref.shape[1] // parts // 2
    core = lax.rem(place_ref[0], 2)
    for part in range(parts):
        first = part * (2 * half)
        for out, side in ((mine_out, core), (other_out, 1 - core)):
            out[part * half : (part + 1) * half, :] = panel_ref[
                0, pl.ds(pl.multiple_of(first + side * half, 16), half), :
            ]


def rows_kernel(groups, capacity, points_ref, partner_ref, tags_ref, halves_ref, out_ref, marks_ref):
    half, marks = halves_ref.shape[1], marks_ref.shape[0]
    slots = points_ref.shape[0]
    tag_lanes = tags_ref.shape[1]
    for part in range(halves_ref.shape[0]):
        marks_ref[part * half : (part + 1) * half, :] = unit_rows(halves_ref[part])
    for core, (placed, tags) in enumerate(
        ((points_ref, tags_ref[...]), (partner_ref, jnp.zeros((slots, tag_lanes), jnp.bfloat16)))
    ):
        scores = lax.dot_general(placed[...], marks_ref[...], NT, preferred_element_type=jnp.float32)
        rows = jnp.exp(scores * (0.5 / math.sqrt(placed.shape[1]))).astype(jnp.bfloat16)
        if len(out_ref.shape) == 4:
            for group in range(groups):
                here = slice(group * capacity, (group + 1) * capacity)
                out_ref[group, core, :, :marks] = rows[here]
                out_ref[group, core, :, marks:] = tags[here]
        else:
            out_ref[core, :, :marks] = rows
            out_ref[core, :, marks:] = tags


def sums_kernel(scale, even_ref, odd_ref, *refs):
    blocks, totals_ref, counts_ref, panel_ref = refs[:-3], refs[-3], refs[-2], refs[-1]
    slots, lanes = even_ref.shape
    owned = totals_ref.shape[0]
    for side in range(2):
        first = 0
        for block in blocks[side * len(blocks) // 2 : (side + 1) * len(blocks) // 2]:
            panel_ref[side, first : first + block.shape[0], :] = block[...]
            first += block.shape[0]
        marks = first
        panel_ref[side, marks:, :] = jnp.zeros((lanes - marks, panel_ref.shape[2]), jnp.bfloat16)
    features = (
        jnp.dot(even_ref[...], panel_ref[0], preferred_element_type=jnp.float32)
        + jnp.dot(odd_ref[...], panel_ref[1], preferred_element_type=jnp.float32)
    ).astype(jnp.bfloat16)
    which = lax.broadcasted_iota(jnp.int32, (8, lanes - marks), 1)
    weights = jnp.where(which == 0, 256.0, jnp.where(which == 1, 1.0, 0.0)).astype(jnp.bfloat16)
    tags = lax.dot_general(weights, even_ref[:, marks:], NT, preferred_element_type=jnp.float32)
    tags += lax.dot_general(weights, odd_ref[:, marks:], NT, preferred_element_type=jnp.float32)
    tags = tags[:1].astype(jnp.int32)
    member = (
        (lax.broadcasted_iota(jnp.int32, (owned, slots), 0) + 1 == tags)
        .astype(jnp.float32)
        .astype(jnp.bfloat16)
    )
    totals_ref[...] = jnp.dot(member, features, preferred_element_type=jnp.float32) * scale
    counts_ref[...] = lax.dot_general(
        jnp.ones((8, slots), jnp.bfloat16), member, NT, preferred_element_type=jnp.float32
    )[:1].astype(jnp.int32)


def call(kernel, shapes, *operands, place=None, scratch=()):
    whole = pl.BlockSpec(memory_space=pltpu.VMEM)
    many = isinstance(shapes, tuple)
    scalar = [] if place is None else [place]
    return pl.pallas_call(
        kernel,
        out_shape=shapes,
        in_specs=[pl.BlockSpec(memory_space=pltpu.SMEM)] * len(scalar) + [whole] * len(operands),
        out_specs=(whole,) * len(shapes) if many else whole,
        scratch_shapes=scratch,
        compiler_params=pltpu.CompilerParams(vmem_limit_bytes=VMEM_LIMIT),
    )(*scalar, *operands)


def array(shape, dtype=jnp.bfloat16):
    return jax.ShapeDtypeStruct(shape, dtype)


def swap(block, axis, mask):
    return lax.ppermute(block, axis, [(i, i ^ mask) for i in range(lax.axis_size(axis))])


def gather(block, axis):
    size = lax.axis_size(axis)
    return lax.all_to_all(
        jnp.broadcast_to(block[None], (size,) + block.shape), axis, split_axis=0, concat_axis=0, tiled=True
    )


def spread(mine, other, holder, groups):
    me = lax.axis_index("pts")

    def pick(block, mask):
        return jnp.where(((holder ^ me) & mask) == 0, block, swap(block, "pts", mask))

    mine = jnp.where(((holder ^ me) & 1) == 0, mine, swap(other, "pts", 1))
    masks = [1 << bit for bit in range(1, groups.bit_length() - 1)]
    size = mine.shape[0] // len(masks)
    blocks = [mine[at * size : (at + 1) * size] for at in range(len(masks))]
    for turn in range(len(masks)):
        blocks = [
            pick(block, masks[(at + turn) % len(masks)]) for at, block in enumerate(blocks)
        ]
    return blocks + [swap(block, "pts", 1) for block in blocks]


def exchange(rows, groups, capacity):
    slots, lanes = groups * capacity, rows.shape[-1]
    if rows.ndim == 3:
        rows = rows.reshape(2, groups, capacity, lanes).swapaxes(0, 1)
    arrived = lax.all_to_all(
        rows.reshape(groups, 2 * capacity, lanes), "pts", split_axis=0, concat_axis=0, tiled=True
    ).reshape(groups // 2, 2, 2 * capacity, lanes)
    core = lax.axis_index("pts") % 2
    even = lax.dynamic_index_in_dim(arrived, core, 1, keepdims=False)
    odd = lax.dynamic_index_in_dim(arrived, 1 - core, 1, keepdims=False)
    odd = jnp.concatenate([odd[:, capacity:], odd[:, :capacity]], axis=1)
    return even.reshape(slots, lanes), odd.reshape(slots, lanes)


def body(points, landmarks, panels, panel_index, assignment):
    groups, parts = lax.axis_size("pts"), lax.axis_size("lmk")
    point_rows, width = points.shape
    capacity = 2 * point_rows // groups
    slots = groups * capacity
    owned = CLUSTERS // groups
    depth, columns = panels.shape[1:]
    half = landmarks.shape[0] // 2
    lanes = -(-(depth // 2 + 2) // LANES) * LANES
    place = jnp.stack([lax.axis_index("pts"), lax.axis_index("lmk")]).astype(jnp.int32)
    mine = lax.dynamic_slice_in_dim(landmarks, (place[0] % 2) * half, half, 0)
    halves = gather(mine, "lmk")
    placed, tags, panel_mine, panel_other = call(
        lambda *refs: place_kernel(groups, capacity, parts, *refs),
        (
            array((slots, width)),
            array((slots, lanes - depth // 2)),
            array((depth // 2, columns)),
            array((depth // 2, columns)),
        ),
        points,
        assignment.reshape(1, point_rows),
        panels,
        place=place,
    )
    partner = swap(placed, "pts", 1)
    blocks = spread(panel_mine, panel_other, panel_index[0], groups)
    rows = call(
        lambda *refs: rows_kernel(groups, capacity, *refs),
        array((groups, 2, capacity, lanes) if capacity % 16 == 0 else (2, slots, lanes)),
        placed,
        partner,
        tags,
        halves,
        scratch=[pltpu.VMEM((depth // 2, width), jnp.bfloat16)],
    )
    even, odd = exchange(rows, groups, capacity)
    totals, counts = call(
        lambda *refs: sums_kernel(CLUSTERS / (point_rows * groups), *refs),
        (array((owned, columns), jnp.float32), array((1, owned), jnp.int32)),
        even,
        odd,
        *blocks,
        scratch=[pltpu.VMEM((2, lanes, columns), jnp.bfloat16)],
    )
    return (totals, counts.reshape(owned))


def solution(mesh):
    in_specs = (P("pts", None), P("lmk", None), P("pts", None, "lmk"), P(), P("pts"))
    out_specs = (P("pts", "lmk"), P("pts"))
    return jax.shard_map(body, mesh=mesh, in_specs=in_specs, out_specs=out_specs, check_vma=False)
```

profile of v0, /device:TPU:0, one launch (start us, length us, event | category | flops | bytes accessed | tf_op | source)
XLA Modules:
  0.0 38.9 jit_solution(17334918056564846627)
XLA Ops:
  0.6 0.0 copy-start
  0.6 0.1 pad_add_fusion.refs_0_
  0.7 0.7 %copy-done.3 = s32[256]{0:T(256)S(1)} copy-done((s32[256]{0:T(256)S(1)}, s32[256]{0:T(256)}, u32[]{:S(2)}) %copy-start.3) | copy-done | bytes 1048
  1.4 1.0 %copy-done.1 = bf16[256,768]{1,0:T(8,128)(2,1)S(1)} copy-done((bf16[256,768]{1,0:T(8,128)(2,1)S(1)}, bf16[256,768]{1,0:T(8,128)(2,1)}, u32[]{:S(2)}) %copy-start.1) | copy-done | bytes 393240
  2.4 1.0 %copy-done.2 = bf16[1,384,512]{2,1,0:T(8,128)(2,1)S(1)} copy-done((bf16[1,384,512]{2,1,0:T(8,128)(2,1)S(1)}, bf16[1,384,512]{2,1,0:T(8,128)(2,1)}, u32[]{:S(2)}) %copy-start.2) | copy-done | bytes 393240
  3.4 1.2 %shard_map.68 = (bf16[512,768]{1,0:T(8,128)(2,1)S(1)}, bf16[512,64]{1,0:T(8,128)(2,1)S(1)}, bf16[192,512]{1,0:T(8,128)(2,1)S(1)}, bf16[192,512]{1,0:T(8,128)(2,1)S(1)}) custom-call(s32[2]{0:T(128)S(1)} %pad_add_fusion.refs_0_, bf16[256,768]{1,0:T(8,128)(2,1)S(1)} %copy-done.1, s32[1,256]{1,0:T(1,128)S(1)} %bitcast.14, bf16[1,384,512]{2,1,0:T(8,128)(2,1)S(1)} %copy-done.2), custom_call_target="tpu_custom_call" | custom-call | tf_op jit(solution)/shard_map/pallas_call | solution.py:123
  4.6 0.5 %collective-permute-start.1 = (bf16[192,512]{1,0:T(8,128)(2,1)S(1)}, bf16[192,512]{1,0:T(8,128)(2,1)S(1)}, u32[]{:S(2)}, u32[]{:S(2)}) collective-permute-start(bf16[192,512]{1,0:T(8,128)(2,1)S(1)} %get-tuple-element.11), channel_id=1, source_target_pairs={{0,4},{4,0},{8,12},{12,8},{16,20},{20,16},{24,28},{28,24},{1,5},{5... | collective-permute-start | bytes 589832 | tf_op jit(solution)/shard_map/ppermute | solution.py:138
  5.1 0.7 %broadcast_in_dim.2 = bf16[4,48,768]{2,1,0:T(8,128)(2,1)} broadcast(bf16[48,768]{1,0:T(8,128)(2,1)S(1)} %constant_dynamic-slice_fusion.1), dimensions={1,2} | broadcast | bytes 368640 | tf_op jit(solution)/shard_map/broadcast_in_dim | solution.py:144
  5.8 5.9 %all-to-all-start = ((bf16[4,48,768]{2,1,0:T(8,128)(2,1)}), bf16[4,48,768]{2,1,0:T(8,128)(2,1)S(1)}, u32[]{:S(2)}, u32[]{:S(2)}) async-start(bf16[4,48,768]{2,1,0:T(8,128)(2,1)} %broadcast_in_dim.2), calls=%async_computation | async-start | bytes 589824 | tf_op jit(solution)/shard_map/all_to_all | solution.py:143
  11.7 0.2 collective-permute-start
  12.6 1.6 %collective-permute-start.2 = (bf16[96,512]{1,0:T(8,128)(2,1)S(1)}, bf16[96,512]{1,0:T(8,128)(2,1)S(1)}, u32[]{:S(2)}, u32[]{:S(2)}) collective-permute-start(bf16[96,512]{1,0:T(8,128)(2,1)S(1)} %get-tuple-element.21), channel_id=1, source_target_pairs={{0,8},{4,12},{8,0},{12,4},{16,24},{20,28},{24,16},{28,20},{1,9},{5... | collective-permute-start | bytes 294920 | tf_op jit(solution)/shard_map/ppermute | solution.py:138
  14.2 1.5 %collective-permute-start.4 = (bf16[96,512]{1,0:T(8,128)(2,1)S(1)}, bf16[96,512]{1,0:T(8,128)(2,1)S(1)}, u32[]{:S(2)}, u32[]{:S(2)}) collective-permute-start(bf16[96,512]{1,0:T(8,128)(2,1)S(1)} %get-tuple-element.20), channel_id=1, source_target_pairs={{0,16},{4,20},{8,24},{12,28},{16,0},{20,4},{24,8},{28,12},{1,17},{... | collective-permute-start | bytes 294920 | tf_op jit(solution)/shard_map/ppermute | solution.py:138
  15.7 2.0 %collective-permute-done.2 = bf16[96,512]{1,0:T(8,128)(2,1)S(1)} collective-permute-done((bf16[96,512]{1,0:T(8,128)(2,1)S(1)}, bf16[96,512]{1,0:T(8,128)(2,1)S(1)}, u32[]{:S(2)}, u32[]{:S(2)}) %collective-permute-start.2) | collective-permute-done | bytes 98336 | tf_op jit(solution)/shard_map/ppermute | solution.py:138
  17.7 1.2 %collective-permute-done.4 = bf16[96,512]{1,0:T(8,128)(2,1)S(1)} collective-permute-done((bf16[96,512]{1,0:T(8,128)(2,1)S(1)}, bf16[96,512]{1,0:T(8,128)(2,1)S(1)}, u32[]{:S(2)}, u32[]{:S(2)}) %collective-permute-start.4) | collective-permute-done | bytes 98336 | tf_op jit(solution)/shard_map/ppermute | solution.py:138
  19.0 0.6 %collective-permute-start.5 = (bf16[96,512]{1,0:T(8,128)(2,1)S(1)}, bf16[96,512]{1,0:T(8,128)(2,1)S(1)}, u32[]{:S(2)}, u32[]{:S(2)}) collective-permute-start(bf16[96,512]{1,0:T(8,128)(2,1)S(1)} %get-tuple-element.18), channel_id=1, source_target_pairs={{0,8},{4,12},{8,0},{12,4},{16,24},{20,28},{24,16},{28,20},{1,9},{5... | collective-permute-start | bytes 294920 | tf_op jit(solution)/shard_map/ppermute | solution.py:138
  19.6 1.5 %collective-permute-start.3 = (bf16[96,512]{1,0:T(8,128)(2,1)S(1)}, bf16[96,512]{1,0:T(8,128)(2,1)S(1)}, u32[]{:S(2)}, u32[]{:S(2)}) collective-permute-start(bf16[96,512]{1,0:T(8,128)(2,1)S(1)} %get-tuple-element.19), channel_id=1, source_target_pairs={{0,16},{4,20},{8,24},{12,28},{16,0},{20,4},{24,8},{28,12},{1,17},{... | collective-permute-start | bytes 294920 | tf_op jit(solution)/shard_map/ppermute | solution.py:138
  21.1 0.8 %all-to-all-done.refs_3_ = bf16[4,48,768]{2,1,0:T(8,128)(2,1)S(1)} async-done(((bf16[4,48,768]{2,1,0:T(8,128)(2,1)}), bf16[4,48,768]{2,1,0:T(8,128)(2,1)S(1)}, u32[]{:S(2)}, u32[]{:S(2)}) %all-to-all-start) | async-done | bytes 294944 | tf_op jit(solution)/shard_map/all_to_all | solution.py:143
  21.9 0.0 collective-permute-done.refs_1_
  21.9 1.5 %shard_map.69 = bf16[8,2,64,256]{3,2,1,0:T(8,128)(2,1)} custom-call(bf16[512,768]{1,0:T(8,128)(2,1)S(1)} %get-tuple-element.8.refs_0_, bf16[512,768]{1,0:T(8,128)(2,1)S(1)} %collective-permute-done.refs_1_, bf16[512,64]{1,0:T(8,128)(2,1)S(1)} %get-tuple-element.9.refs_2_, bf16[4,48,768]{2,1,0:T(8,128)(2,1)S(1)} %all-to-all-done.refs_3_), custom_call_target="tpu_custom_call" | custom-call | tf_op jit(solution)/shard_map/pallas_call | solution.py:123
  23.4 3.7 %all-to-all-start.1 = ((bf16[8,128,256]{2,1,0:T(8,128)(2,1)}), bf16[8,128,256]{2,1,0:T(8,128)(2,1)S(1)}, u32[]{:S(2)}, u32[]{:S(2)}) async-start(bf16[8,128,256]{2,1,0:T(8,128)(2,1)} %bitcast.3), calls=%async_computation.1 | async-start | bytes 1048576 | tf_op jit(solution)/shard_map/all_to_all | solution.py:169
  27.2 0.6 %collective-permute-start.7 = (bf16[96,512]{1,0:T(8,128)(2,1)S(1)}, bf16[96,512]{1,0:T(8,128)(2,1)S(1)}, u32[]{:S(2)}, u32[]{:S(2)}) collective-permute-start(bf16[96,512]{1,0:T(8,128)(2,1)S(1)} %broadcast_select_fusion.1.refs_3_), channel_id=1, source_target_pairs={{0,4},{4,0},{8,12},{12,8},{16,20},{20,16},{24,28},{28,24},{1,5},{5... | collective-permute-start | bytes 294920 | tf_op jit(solution)/shard_map/ppermute | solution.py:138
  27.8 0.1 collective-permute-start.6
  27.9 9.0 %all-to-all-done.1 = bf16[8,128,256]{2,1,0:T(8,128)(2,1)S(1)} async-done(((bf16[8,128,256]{2,1,0:T(8,128)(2,1)}), bf16[8,128,256]{2,1,0:T(8,128)(2,1)S(1)}, u32[]{:S(2)}, u32[]{:S(2)}) %all-to-all-start.1) | async-done | bytes 524320 | tf_op jit(solution)/shard_map/all_to_all | solution.py:169
  37.0 1.9 %shard_map.70 = (f32[512,512]{1,0:T(8,128)}, s32[1,512]{1,0:T(1,128)}) custom-call(bf16[512,256]{1,0:T(8,128)(2,1)S(1)} %bitcast.12, bf16[512,256]{1,0:T(8,128)(2,1)S(1)} %bitcast.13, bf16[96,512]{1,0:T(8,128)(2,1)S(1)} %broadcast_select_fusion.4.refs_2_, bf16[96,512]{1,0:T(8,128)(2,1)S(1)} %broadcast_select_fusion.1.refs_3_, ...), custom_call_target="tpu_custom_call" | custom-call | tf_op jit(solution)/shard_map/pallas_call | solution.py:123
  (18 shorter events, 0.2 us)
Async XLA Ops:
  0.6 4.5 %copy-start = (bf16[96,768]{1,0:T(8,128)(2,1)S(1)}, bf16[96,768]{1,0:T(8,128)(2,1)}, u32[]{:S(2)}) copy-start(bf16[96,768]{1,0:T(8,128)(2,1)} %param.6) | copy-start | bytes 442372
  0.7 0.7 %copy-start.3 = (s32[256]{0:T(256)S(1)}, s32[256]{0:T(256)}, u32[]{:S(2)}) copy-start(s32[256]{0:T(256)} %param.9) | copy-start | bytes 3076
  1.4 1.0 %copy-start.1 = (bf16[256,768]{1,0:T(8,128)(2,1)S(1)}, bf16[256,768]{1,0:T(8,128)(2,1)}, u32[]{:S(2)}) copy-start(bf16[256,768]{1,0:T(8,128)(2,1)} %refs_1_.1) | copy-start | bytes 1179652
  2.4 1.0 %copy-start.2 = (bf16[1,384,512]{2,1,0:T(8,128)(2,1)S(1)}, bf16[1,384,512]{2,1,0:T(8,128)(2,1)}, u32[]{:S(2)}) copy-start(bf16[1,384,512]{2,1,0:T(8,128)(2,1)} %refs_3_.1) | copy-start | bytes 1179652
  4.6 8.0 %collective-permute-start.1 = (bf16[192,512]{1,0:T(8,128)(2,1)S(1)}, bf16[192,512]{1,0:T(8,128)(2,1)S(1)}, u32[]{:S(2)}, u32[]{:S(2)}) collective-permute-start(bf16[192,512]{1,0:T(8,128)(2,1)S(1)} %get-tuple-element.11), channel_id=1, source_target_pairs={{0,4},{4,0},{8,12},{12,8},{16,20},{20,16},{24,28},{28,24},{1,5},{5... | collective-permute-start | bytes 589832 | tf_op jit(solution)/shard_map/ppermute | solution.py:138
  5.8 16.1 %all-to-all-start = ((bf16[4,48,768]{2,1,0:T(8,128)(2,1)}), bf16[4,48,768]{2,1,0:T(8,128)(2,1)S(1)}, u32[]{:S(2)}, u32[]{:S(2)}) async-start(bf16[4,48,768]{2,1,0:T(8,128)(2,1)} %broadcast_in_dim.2), calls=%async_computation | async-start | bytes 589824 | tf_op jit(solution)/shard_map/all_to_all | solution.py:143
  11.7 10.2 %collective-permute-start = (bf16[512,768]{1,0:T(8,128)(2,1)S(1)}, bf16[512,768]{1,0:T(8,128)(2,1)S(1)}, u32[]{:S(2)}, u32[]{:S(2)}) collective-permute-start(bf16[512,768]{1,0:T(8,128)(2,1)S(1)} %get-tuple-element.8.refs_0_), channel_id=1, source_target_pairs={{0,4},{4,0},{8,12},{12,8},{16,20},{20,16},{24,28},{28,24},{1,5},{5... | collective-permute-start | bytes 2359304 | tf_op jit(solution)/shard_map/ppermute | solution.py:138
  12.6 5.1 %collective-permute-start.2 = (bf16[96,512]{1,0:T(8,128)(2,1)S(1)}, bf16[96,512]{1,0:T(8,128)(2,1)S(1)}, u32[]{:S(2)}, u32[]{:S(2)}) collective-permute-start(bf16[96,512]{1,0:T(8,128)(2,1)S(1)} %get-tuple-element.21), channel_id=1, source_target_pairs={{0,8},{4,12},{8,0},{12,4},{16,24},{20,28},{24,16},{28,20},{1,9},{5... | collective-permute-start | bytes 294920 | tf_op jit(solution)/shard_map/ppermute | solution.py:138
  14.2 4.7 %collective-permute-start.4 = (bf16[96,512]{1,0:T(8,128)(2,1)S(1)}, bf16[96,512]{1,0:T(8,128)(2,1)S(1)}, u32[]{:S(2)}, u32[]{:S(2)}) collective-permute-start(bf16[96,512]{1,0:T(8,128)(2,1)S(1)} %get-tuple-element.20), channel_id=1, source_target_pairs={{0,16},{4,20},{8,24},{12,28},{16,0},{20,4},{24,8},{28,12},{1,17},{... | collective-permute-start | bytes 294920 | tf_op jit(solution)/shard_map/ppermute | solution.py:138
  19.0 8.2 %collective-permute-start.5 = (bf16[96,512]{1,0:T(8,128)(2,1)S(1)}, bf16[96,512]{1,0:T(8,128)(2,1)S(1)}, u32[]{:S(2)}, u32[]{:S(2)}) collective-permute-start(bf16[96,512]{1,0:T(8,128)(2,1)S(1)} %get-tuple-element.18), channel_id=1, source_target_pairs={{0,8},{4,12},{8,0},{12,4},{16,24},{20,28},{24,16},{28,20},{1,9},{5... | collective-permute-start | bytes 294920 | tf_op jit(solution)/shard_map/ppermute | solution.py:138
  19.6 8.2 %collective-permute-start.3 = (bf16[96,512]{1,0:T(8,128)(2,1)S(1)}, bf16[96,512]{1,0:T(8,128)(2,1)S(1)}, u32[]{:S(2)}, u32[]{:S(2)}) collective-permute-start(bf16[96,512]{1,0:T(8,128)(2,1)S(1)} %get-tuple-element.19), channel_id=1, source_target_pairs={{0,16},{4,20},{8,24},{12,28},{16,0},{20,4},{24,8},{28,12},{1,17},{... | collective-permute-start | bytes 294920 | tf_op jit(solution)/shard_map/ppermute | solution.py:138
  23.4 13.5 %all-to-all-start.1 = ((bf16[8,128,256]{2,1,0:T(8,128)(2,1)}), bf16[8,128,256]{2,1,0:T(8,128)(2,1)S(1)}, u32[]{:S(2)}, u32[]{:S(2)}) async-start(bf16[8,128,256]{2,1,0:T(8,128)(2,1)} %bitcast.3), calls=%async_computation.1 | async-start | bytes 1048576 | tf_op jit(solution)/shard_map/all_to_all | solution.py:169
  27.2 9.8 %collective-permute-start.7 = (bf16[96,512]{1,0:T(8,128)(2,1)S(1)}, bf16[96,512]{1,0:T(8,128)(2,1)S(1)}, u32[]{:S(2)}, u32[]{:S(2)}) collective-permute-start(bf16[96,512]{1,0:T(8,128)(2,1)S(1)} %broadcast_select_fusion.1.refs_3_), channel_id=1, source_target_pairs={{0,4},{4,0},{8,12},{12,8},{16,20},{20,16},{24,28},{28,24},{1,5},{5... | collective-permute-start | bytes 294920 | tf_op jit(solution)/shard_map/ppermute | solution.py:138
  27.8 9.2 %collective-permute-start.6 = (bf16[96,512]{1,0:T(8,128)(2,1)S(1)}, bf16[96,512]{1,0:T(8,128)(2,1)S(1)}, u32[]{:S(2)}, u32[]{:S(2)}) collective-permute-start(bf16[96,512]{1,0:T(8,128)(2,1)S(1)} %broadcast_select_fusion.4.refs_2_), channel_id=1, source_target_pairs={{0,4},{4,0},{8,12},{12,8},{16,20},{20,16},{24,28},{28,24},{1,5},{5... | collective-permute-start | bytes 294920 | tf_op jit(solution)/shard_map/ppermute | solution.py:138
where the time goes:
time: 39.3 us; the launch traced here: 38.9 us
  starting transfers between devices  16.2 us (41%)
  waiting for transfers between devices  13.1 us (33%)
  Pallas kernels  4.55 us (12%)
  local copies, waits for them, and re-layouts  3.49 us (9%)
  between operations  1.4 us (4%)
    all_to_all x1, waiting for transfers between devices, exchange(): lax.all_to_all(rows.reshape(groups, 2 * capacity, lanes), 'pts', split_ax...  9.04 us
    ppermute x8, starting transfers between devices, swap(): lax.ppermute(block, axis, [(i, i ^ mask) for i in range(lax.axis_size(axi...  6.55 us
    all_to_all x1, starting transfers between devices, gather(): lax.all_to_all(jnp.broadcast_to(block[None], (size,) + block.shape), axis...  5.91 us
    pallas_call x3, Pallas kernels, call(): pl.pallas_call(kernel, out_shape=shapes, in_specs=[pl.BlockSpec(memory_sp...  4.55 us
    all_to_all x1, starting transfers between devices, exchange(): lax.all_to_all(rows.reshape(groups, 2 * capacity, lanes), 'pts', split_ax...  3.72 us
    ppermute x8, waiting for transfers between devices, swap(): lax.ppermute(block, axis, [(i, i ^ mask) for i in range(lax.axis_size(axi...  3.24 us
    unnamed x8, local copies, waits for them, and re-layouts  2.68 us
    all_to_all x1, waiting for transfers between devices, gather(): lax.all_to_all(jnp.broadcast_to(block[None], (size,) + block.shape), axis...  0.84 us
  transfers between devices with their start and end apart: 10, of which 4 were waited for; matrix products, arithmetic and copies ran while one was open for 2% of the time, Pallas kernels for 4%

commit v1 on v0

--- a/solution.py
+++ b/solution.py
@@ -19,8 +19,31 @@
     return (widened * scale).astype(jnp.bfloat16)
 
 
-def place_kernel(groups, capacity, parts, place_ref, points_ref, assignment_ref, panel_ref, *outs):
-    points_out, tags_out, mine_out, other_out = outs
+def fetch_kernel(place_ref, points_ref, marks_ref, assignment_ref, panel_ref, *refs):
+    points_out, halves_out, assignment_out, mine_out, other_out, sems = refs
+    parts, half = halves_out.shape[:2]
+    core = lax.rem(place_ref[0], 2)
+    pairs = [(points_ref, points_out), (assignment_ref, assignment_out)]
+    for part in range(parts):
+        pairs.append(
+            (marks_ref.at[pl.ds(pl.multiple_of(core * half, 16), half), :], halves_out.at[part])
+        )
+        for out, side in ((mine_out, core), (other_out, 1 - core)):
+            first = pl.multiple_of((2 * part + side) * half, 16)
+            pairs.append(
+                (
+                    panel_ref.at[0, pl.ds(first, half), :],
+                    out.at[part * half : (part + 1) * half, :],
+                )
+            )
+    copies = [pltpu.make_async_copy(*pair, sems.at[at]) for at, pair in enumerate(pairs)]
+    for copy in copies:
+        copy.start()
+    for copy in copies:
+        copy.wait()
+
+
+def place_kernel(groups, capacity, points_ref, assignment_ref, points_out, tags_out):
     point_rows = points_ref.shape[0]
     ids = assignment_ref[...]
     owned = CLUSTERS // groups
@@ -54,14 +77,6 @@
         NT,
         preferred_element_type=jnp.float32,
     ).astype(jnp.bfloat16)
-    half = panel_ref.shape[1] // parts // 2
-    core = lax.rem(place_ref[0], 2)
-    for part in range(parts):
-        first = part * (2 * half)
-        for out, side in ((mine_out, core), (other_out, 1 - core)):
-            out[part * half : (part + 1) * half, :] = panel_ref[
-                0, pl.ds(pl.multiple_of(first + side * half, 16), half), :
-            ]
 
 
 def rows_kernel(groups, capacity, points_ref, partner_ref, tags_ref, halves_ref, out_ref, marks_ref):
@@ -116,14 +131,15 @@
     )[:1].astype(jnp.int32)
 
 
-def call(kernel, shapes, *operands, place=None, scratch=()):
+def call(kernel, shapes, *operands, place=None, scratch=(), kept=False):
     whole = pl.BlockSpec(memory_space=pltpu.VMEM)
     many = isinstance(shapes, tuple)
     scalar = [] if place is None else [place]
     return pl.pallas_call(
         kernel,
         out_shape=shapes,
-        in_specs=[pl.BlockSpec(memory_space=pltpu.SMEM)] * len(scalar) + [whole] * len(operands),
+        in_specs=[pl.BlockSpec(memory_space=pltpu.SMEM)] * len(scalar)
+        + [pl.BlockSpec(memory_space=pl.ANY) if kept else whole] * len(operands),
         out_specs=(whole,) * len(shapes) if many else whole,
         scratch_shapes=scratch,
         compiler_params=pltpu.CompilerParams(vmem_limit_bytes=VMEM_LIMIT),
@@ -136,13 +152,6 @@
 
 def swap(block, axis, mask):
     return lax.ppermute(block, axis, [(i, i ^ mask) for i in range(lax.axis_size(axis))])
-
-
-def gather(block, axis):
-    size = lax.axis_size(axis)
-    return lax.all_to_all(
-        jnp.broadcast_to(block[None], (size,) + block.shape), axis, split_axis=0, concat_axis=0, tiled=True
-    )
 
 
 def spread(mine, other, holder, groups):
@@ -186,20 +195,29 @@
     half = landmarks.shape[0] // 2
     lanes = -(-(depth // 2 + 2) // LANES) * LANES
     place = jnp.stack([lax.axis_index("pts"), lax.axis_index("lmk")]).astype(jnp.int32)
-    mine = lax.dynamic_slice_in_dim(landmarks, (place[0] % 2) * half, half, 0)
-    halves = gather(mine, "lmk")
-    placed, tags, panel_mine, panel_other = call(
-        lambda *refs: place_kernel(groups, capacity, parts, *refs),
+    points, halves, assignment, panel_mine, panel_other = call(
+        fetch_kernel,
         (
-            array((slots, width)),
-            array((slots, lanes - depth // 2)),
+            array((point_rows, width)),
+            array((parts, half, width)),
+            array((1, point_rows), jnp.int32),
             array((depth // 2, columns)),
             array((depth // 2, columns)),
         ),
         points,
+        landmarks,
         assignment.reshape(1, point_rows),
         panels,
         place=place,
+        scratch=[pltpu.SemaphoreType.DMA((3 * parts + 2,))],
+        kept=True,
+    )
+    halves = lax.all_to_all(halves, "lmk", split_axis=0, concat_axis=0, tiled=True)
+    placed, tags = call(
+        lambda *refs: place_kernel(groups, capacity, *refs),
+        (array((slots, width)), array((slots, lanes - depth // 2))),
+        points,
+        assignment,
     )
     partner = swap(placed, "pts", 1)
     blocks = spread(panel_mine, panel_other, panel_index[0], groups)

time: 39.3 us -> 41.6 us (1.059)
  Pallas kernels: 4.55 us -> 6.5 us
    pallas_call x3 -> x4, Pallas kernels: 4.55 us -> 6.5 us  [call(): pl.pallas_call(kernel, out_shape=shapes, in_specs=[pl.BlockSpec(memory_sp...]
    unnamed x8, local copies, waits for them, and re-layouts: 2.68 us -> 3.58 us
    broadcast_in_dim x1 -> x0, local copies, waits for them, and re-layouts: 0.73 us -> none  [gather(): jnp.broadcast_to(block[None], (size,) + block.shape)]
  transfers between devices with their start and end apart: 10 -> 10, of which waited for: 4 -> 4; matrix products, arithmetic and copies ran while one was open for 2% -> 0% of each run, Pallas kernels for 4% -> 5%
where the time goes in v1:
time: 41.6 us; the launch traced here: 41.2 us
  starting transfers between devices  16.5 us (40%)
  waiting for transfers between devices  13 us (31%)
  Pallas kernels  6.5 us (16%)
  local copies, waits for them, and re-layouts  3.65 us (9%)
  between operations  1.39 us (3%)
    all_to_all x1, waiting for transfers between devices, exchange(): lax.all_to_all(rows.reshape(groups, 2 * capacity, lanes), 'pts', split_ax...  9.04 us
    pallas_call x4, Pallas kernels, call(): pl.pallas_call(kernel, out_shape=shapes, in_specs=[pl.BlockSpec(memory_sp...  6.5 us
    ppermute x8, starting transfers between devices, swap(): lax.ppermute(block, axis, [(i, i ^ mask) for i in range(lax.axis_size(axi...  6.43 us
    all_to_all x1, starting transfers between devices, body(): lax.all_to_all(halves, 'lmk', split_axis=0, concat_axis=0, tiled=True)  6.32 us
    all_to_all x1, starting transfers between devices, exchange(): lax.all_to_all(rows.reshape(groups, 2 * capacity, lanes), 'pts', split_ax...  3.72 us
    unnamed x8, local copies, waits for them, and re-layouts  3.58 us
    ppermute x8, waiting for transfers between devices, swap(): lax.ppermute(block, axis, [(i, i ^ mask) for i in range(lax.axis_size(axi...  3.14 us
  transfers between devices with their start and end apart: 10, of which 4 were waited for; matrix products, arithmetic and copies ran while one was open for 0% of the time, Pallas kernels for 5%

profile of v1, /device:TPU:0, one launch (start us, length us, event | category | flops | bytes accessed | tf_op | source)
XLA Modules:
  0.0 41.2 jit_solution(15713429417635949009)
XLA Ops:
  0.6 0.1 pad_add_fusion.place_ref
  0.7 0.7 %copy-done.3 = s32[256]{0:T(256)S(1)} copy-done((s32[256]{0:T(256)S(1)}, s32[256]{0:T(256)}, u32[]{:S(2)}) %copy-start.3) | copy-done | bytes 1048
  1.4 1.0 %copy-done = bf16[256,768]{1,0:T(8,128)(2,1)S(1)} copy-done((bf16[256,768]{1,0:T(8,128)(2,1)S(1)}, bf16[256,768]{1,0:T(8,128)(2,1)}, u32[]{:S(2)}) %copy-start) | copy-done | bytes 393240
  2.4 1.0 %copy-done.1 = bf16[1,384,512]{2,1,0:T(8,128)(2,1)S(1)} copy-done((bf16[1,384,512]{2,1,0:T(8,128)(2,1)S(1)}, bf16[1,384,512]{2,1,0:T(8,128)(2,1)}, u32[]{:S(2)}) %copy-start.1) | copy-done | bytes 393240
  3.4 0.9 %copy-done.2 = bf16[96,768]{1,0:T(8,128)(2,1)S(1)} copy-done((bf16[96,768]{1,0:T(8,128)(2,1)S(1)}, bf16[96,768]{1,0:T(8,128)(2,1)}, u32[]{:S(2)}) %copy-start.2) | copy-done | bytes 147480
  4.3 2.5 %shard_map.68 = (bf16[256,768]{1,0:T(8,128)(2,1)S(1)}, bf16[4,48,768]{2,1,0:T(8,128)(2,1)}, s32[1,256]{1,0:T(1,128)S(1)}, bf16[192,512]{1,0:T(8,128)(2,1)S(1)}, bf16[192,512]{1,0:T(8,128)(2,1)S(1)}) custom-call(s32[2]{0:T(128)S(1)} %pad_add_fusion.place_ref, bf16[256,768]{1,0:T(8,128)(2,1)S(1)} %copy-done, bf16[96,768]{1,0:T(8,128)(2,1)S(1)} %copy-done.2, ...), custom_call_target="tpu_custom_call" | custom-call | tf_op jit(solution)/shard_map/pallas_call | solution.py:138
  6.8 0.5 %collective-permute-start.1 = (bf16[192,512]{1,0:T(8,128)(2,1)S(1)}, bf16[192,512]{1,0:T(8,128)(2,1)S(1)}, u32[]{:S(2)}, u32[]{:S(2)}) collective-permute-start(bf16[192,512]{1,0:T(8,128)(2,1)S(1)} %get-tuple-element.17), channel_id=1, source_target_pairs={{0,4},{4,0},{8,12},{12,8},{16,20},{20,16},{24,28},{28,24},{1,5},{5... | collective-permute-start | bytes 589832 | tf_op jit(solution)/shard_map/ppermute | solution.py:154
  7.3 0.6 %shard_map.69 = (bf16[512,768]{1,0:T(8,128)(2,1)S(1)}, bf16[512,64]{1,0:T(8,128)(2,1)S(1)}) custom-call(bf16[256,768]{1,0:T(8,128)(2,1)S(1)} %get-tuple-element.11.refs_0_, s32[1,256]{1,0:T(1,128)S(1)} %get-tuple-element.12.refs_1_), custom_call_target="tpu_custom_call" | custom-call | tf_op jit(solution)/shard_map/pallas_call | solution.py:138
  7.9 0.1 collective-permute-start
  8.1 6.3 %all-to-all-start = ((bf16[4,48,768]{2,1,0:T(8,128)(2,1)}), bf16[4,48,768]{2,1,0:T(8,128)(2,1)S(1)}, u32[]{:S(2)}, u32[]{:S(2)}) async-start(bf16[4,48,768]{2,1,0:T(8,128)(2,1)} %get-tuple-element.15), calls=%async_computation | async-start | bytes 589824 | tf_op jit(solution)/shard_map/all_to_all | solution.py:215
  15.0 0.0 collective-permute-done.1
  15.1 1.6 %collective-permute-start.4 = (bf16[96,512]{1,0:T(8,128)(2,1)S(1)}, bf16[96,512]{1,0:T(8,128)(2,1)S(1)}, u32[]{:S(2)}, u32[]{:S(2)}) collective-permute-start(bf16[96,512]{1,0:T(8,128)(2,1)S(1)} %get-tuple-element.26), channel_id=1, source_target_pairs={{0,16},{4,20},{8,24},{12,28},{16,0},{20,4},{24,8},{28,12},{1,17},{... | collective-permute-start | bytes 294920 | tf_op jit(solution)/shard_map/ppermute | solution.py:154
  16.7 1.5 %collective-permute-start.2 = (bf16[96,512]{1,0:T(8,128)(2,1)S(1)}, bf16[96,512]{1,0:T(8,128)(2,1)S(1)}, u32[]{:S(2)}, u32[]{:S(2)}) collective-permute-start(bf16[96,512]{1,0:T(8,128)(2,1)S(1)} %get-tuple-element.27), channel_id=1, source_target_pairs={{0,8},{4,12},{8,0},{12,4},{16,24},{20,28},{24,16},{28,20},{1,9},{5... | collective-permute-start | bytes 294920 | tf_op jit(solution)/shard_map/ppermute | solution.py:154
  18.2 1.6 %collective-permute-done.4 = bf16[96,512]{1,0:T(8,128)(2,1)S(1)} collective-permute-done((bf16[96,512]{1,0:T(8,128)(2,1)S(1)}, bf16[96,512]{1,0:T(8,128)(2,1)S(1)}, u32[]{:S(2)}, u32[]{:S(2)}) %collective-permute-start.4) | collective-permute-done | bytes 98336 | tf_op jit(solution)/shard_map/ppermute | solution.py:154
  19.8 1.5 %collective-permute-done.2 = bf16[96,512]{1,0:T(8,128)(2,1)S(1)} collective-permute-done((bf16[96,512]{1,0:T(8,128)(2,1)S(1)}, bf16[96,512]{1,0:T(8,128)(2,1)S(1)}, u32[]{:S(2)}, u32[]{:S(2)}) %collective-permute-start.2) | collective-permute-done | bytes 98336 | tf_op jit(solution)/shard_map/ppermute | solution.py:154
  21.3 0.6 %collective-permute-start.3 = (bf16[96,512]{1,0:T(8,128)(2,1)S(1)}, bf16[96,512]{1,0:T(8,128)(2,1)S(1)}, u32[]{:S(2)}, u32[]{:S(2)}) collective-permute-start(bf16[96,512]{1,0:T(8,128)(2,1)S(1)} %get-tuple-element.25), channel_id=1, source_target_pairs={{0,16},{4,20},{8,24},{12,28},{16,0},{20,4},{24,8},{28,12},{1,17},{... | collective-permute-start | bytes 294920 | tf_op jit(solution)/shard_map/ppermute | solution.py:154
  21.9 1.5 %collective-permute-start.5 = (bf16[96,512]{1,0:T(8,128)(2,1)S(1)}, bf16[96,512]{1,0:T(8,128)(2,1)S(1)}, u32[]{:S(2)}, u32[]{:S(2)}) collective-permute-start(bf16[96,512]{1,0:T(8,128)(2,1)S(1)} %get-tuple-element.24), channel_id=1, source_target_pairs={{0,8},{4,12},{8,0},{12,4},{16,24},{20,28},{24,16},{28,20},{1,9},{5... | collective-permute-start | bytes 294920 | tf_op jit(solution)/shard_map/ppermute | solution.py:154
  23.4 0.8 %all-to-all-done.refs_3_ = bf16[4,48,768]{2,1,0:T(8,128)(2,1)S(1)} async-done(((bf16[4,48,768]{2,1,0:T(8,128)(2,1)}), bf16[4,48,768]{2,1,0:T(8,128)(2,1)S(1)}, u32[]{:S(2)}, u32[]{:S(2)}) %all-to-all-start) | async-done | bytes 294944 | tf_op jit(solution)/shard_map/all_to_all | solution.py:215
  24.2 1.5 %shard_map.70 = bf16[8,2,64,256]{3,2,1,0:T(8,128)(2,1)} custom-call(bf16[512,768]{1,0:T(8,128)(2,1)S(1)} %get-tuple-element.13.refs_0_, bf16[512,768]{1,0:T(8,128)(2,1)S(1)} %collective-permute-done.refs_1_, bf16[512,64]{1,0:T(8,128)(2,1)S(1)} %get-tuple-element.14.refs_2_, bf16[4,48,768]{2,1,0:T(8,128)(2,1)S(1)} %all-to-all-done.refs_3_), custom_call_target="tpu_custom_call" | custom-call | tf_op jit(solution)/shard_map/pallas_call | solution.py:138
  25.7 3.7 %all-to-all-start.1 = ((bf16[8,128,256]{2,1,0:T(8,128)(2,1)}), bf16[8,128,256]{2,1,0:T(8,128)(2,1)S(1)}, u32[]{:S(2)}, u32[]{:S(2)}) async-start(bf16[8,128,256]{2,1,0:T(8,128)(2,1)} %bitcast.3), calls=%async_computation.1 | async-start | bytes 1048576 | tf_op jit(solution)/shard_map/all_to_all | solution.py:178
  29.4 0.6 %collective-permute-start.6 = (bf16[96,512]{1,0:T(8,128)(2,1)S(1)}, bf16[96,512]{1,0:T(8,128)(2,1)S(1)}, u32[]{:S(2)}, u32[]{:S(2)}) collective-permute-start(bf16[96,512]{1,0:T(8,128)(2,1)S(1)} %broadcast_select_fusion.4.refs_2_), channel_id=1, source_target_pairs={{0,4},{4,0},{8,12},{12,8},{16,20},{20,16},{24,28},{28,24},{1,5},{5... | collective-permute-start | bytes 294920 | tf_op jit(solution)/shard_map/ppermute | solution.py:154
  30.0 0.1 collective-permute-start.7
  30.1 9.0 %all-to-all-done.1 = bf16[8,128,256]{2,1,0:T(8,128)(2,1)S(1)} async-done(((bf16[8,128,256]{2,1,0:T(8,128)(2,1)}), bf16[8,128,256]{2,1,0:T(8,128)(2,1)S(1)}, u32[]{:S(2)}, u32[]{:S(2)}) %all-to-all-start.1) | async-done | bytes 524320 | tf_op jit(solution)/shard_map/all_to_all | solution.py:178
  39.3 1.9 %shard_map.71 = (f32[512,512]{1,0:T(8,128)}, s32[1,512]{1,0:T(1,128)}) custom-call(bf16[512,256]{1,0:T(8,128)(2,1)S(1)} %bitcast.12, bf16[512,256]{1,0:T(8,128)(2,1)S(1)} %bitcast.13, bf16[96,512]{1,0:T(8,128)(2,1)S(1)} %broadcast_select_fusion.4.refs_2_, bf16[96,512]{1,0:T(8,128)(2,1)S(1)} %broadcast_select_fusion.1.refs_3_, ...), custom_call_target="tpu_custom_call" | custom-call | tf_op jit(solution)/shard_map/pallas_call | solution.py:138
  (17 shorter events, 0.2 us)
Async XLA Ops:
  0.7 0.7 %copy-start.3 = (s32[256]{0:T(256)S(1)}, s32[256]{0:T(256)}, u32[]{:S(2)}) copy-start(s32[256]{0:T(256)} %param.9) | copy-start | bytes 3076
  1.4 1.0 %copy-start = (bf16[256,768]{1,0:T(8,128)(2,1)S(1)}, bf16[256,768]{1,0:T(8,128)(2,1)}, u32[]{:S(2)}) copy-start(bf16[256,768]{1,0:T(8,128)(2,1)} %points_ref.1) | copy-start | bytes 1179652
  2.4 1.0 %copy-start.1 = (bf16[1,384,512]{2,1,0:T(8,128)(2,1)S(1)}, bf16[1,384,512]{2,1,0:T(8,128)(2,1)}, u32[]{:S(2)}) copy-start(bf16[1,384,512]{2,1,0:T(8,128)(2,1)} %panel_ref.1) | copy-start | bytes 1179652
  3.4 0.9 %copy-start.2 = (bf16[96,768]{1,0:T(8,128)(2,1)S(1)}, bf16[96,768]{1,0:T(8,128)(2,1)}, u32[]{:S(2)}) copy-start(bf16[96,768]{1,0:T(8,128)(2,1)} %marks_ref.1) | copy-start | bytes 442372
  6.8 8.2 %collective-permute-start.1 = (bf16[192,512]{1,0:T(8,128)(2,1)S(1)}, bf16[192,512]{1,0:T(8,128)(2,1)S(1)}, u32[]{:S(2)}, u32[]{:S(2)}) collective-permute-start(bf16[192,512]{1,0:T(8,128)(2,1)S(1)} %get-tuple-element.17), channel_id=1, source_target_pairs={{0,4},{4,0},{8,12},{12,8},{16,20},{20,16},{24,28},{28,24},{1,5},{5... | collective-permute-start | bytes 589832 | tf_op jit(solution)/shard_map/ppermute | solution.py:154
  7.9 16.3 %collective-permute-start = (bf16[512,768]{1,0:T(8,128)(2,1)S(1)}, bf16[512,768]{1,0:T(8,128)(2,1)S(1)}, u32[]{:S(2)}, u32[]{:S(2)}) collective-permute-start(bf16[512,768]{1,0:T(8,128)(2,1)S(1)} %get-tuple-element.13.refs_0_), channel_id=1, source_target_pairs={{0,4},{4,0},{8,12},{12,8},{16,20},{20,16},{24,28},{28,24},{1,5},{5... | collective-permute-start | bytes 2359304 | tf_op jit(solution)/shard_map/ppermute | solution.py:154
  8.1 16.1 %all-to-all-start = ((bf16[4,48,768]{2,1,0:T(8,128)(2,1)}), bf16[4,48,768]{2,1,0:T(8,128)(2,1)S(1)}, u32[]{:S(2)}, u32[]{:S(2)}) async-start(bf16[4,48,768]{2,1,0:T(8,128)(2,1)} %get-tuple-element.15), calls=%async_computation | async-start | bytes 589824 | tf_op jit(solution)/shard_map/all_to_all | solution.py:215
  15.1 4.7 %collective-permute-start.4 = (bf16[96,512]{1,0:T(8,128)(2,1)S(1)}, bf16[96,512]{1,0:T(8,128)(2,1)S(1)}, u32[]{:S(2)}, u32[]{:S(2)}) collective-permute-start(bf16[96,512]{1,0:T(8,128)(2,1)S(1)} %get-tuple-element.26), channel_id=1, source_target_pairs={{0,16},{4,20},{8,24},{12,28},{16,0},{20,4},{24,8},{28,12},{1,17},{... | collective-permute-start | bytes 294920 | tf_op jit(solution)/shard_map/ppermute | solution.py:154
  16.7 4.6 %collective-permute-start.2 = (bf16[96,512]{1,0:T(8,128)(2,1)S(1)}, bf16[96,512]{1,0:T(8,128)(2,1)S(1)}, u32[]{:S(2)}, u32[]{:S(2)}) collective-permute-start(bf16[96,512]{1,0:T(8,128)(2,1)S(1)} %get-tuple-element.27), channel_id=1, source_target_pairs={{0,8},{4,12},{8,0},{12,4},{16,24},{20,28},{24,16},{28,20},{1,9},{5... | collective-permute-start | bytes 294920 | tf_op jit(solution)/shard_map/ppermute | solution.py:154
  21.3 8.1 %collective-permute-start.3 = (bf16[96,512]{1,0:T(8,128)(2,1)S(1)}, bf16[96,512]{1,0:T(8,128)(2,1)S(1)}, u32[]{:S(2)}, u32[]{:S(2)}) collective-permute-start(bf16[96,512]{1,0:T(8,128)(2,1)S(1)} %get-tuple-element.25), channel_id=1, source_target_pairs={{0,16},{4,20},{8,24},{12,28},{16,0},{20,4},{24,8},{28,12},{1,17},{... | collective-permute-start | bytes 294920 | tf_op jit(solution)/shard_map/ppermute | solution.py:154
  21.9 8.1 %collective-permute-start.5 = (bf16[96,512]{1,0:T(8,128)(2,1)S(1)}, bf16[96,512]{1,0:T(8,128)(2,1)S(1)}, u32[]{:S(2)}, u32[]{:S(2)}) collective-permute-start(bf16[96,512]{1,0:T(8,128)(2,1)S(1)} %get-tuple-element.24), channel_id=1, source_target_pairs={{0,8},{4,12},{8,0},{12,4},{16,24},{20,28},{24,16},{28,20},{1,9},{5... | collective-permute-start | bytes 294920 | tf_op jit(solution)/shard_map/ppermute | solution.py:154
  25.7 13.5 %all-to-all-start.1 = ((bf16[8,128,256]{2,1,0:T(8,128)(2,1)}), bf16[8,128,256]{2,1,0:T(8,128)(2,1)S(1)}, u32[]{:S(2)}, u32[]{:S(2)}) async-start(bf16[8,128,256]{2,1,0:T(8,128)(2,1)} %bitcast.3), calls=%async_computation.1 | async-start | bytes 1048576 | tf_op jit(solution)/shard_map/all_to_all | solution.py:178
  29.4 9.8 %collective-permute-start.6 = (bf16[96,512]{1,0:T(8,128)(2,1)S(1)}, bf16[96,512]{1,0:T(8,128)(2,1)S(1)}, u32[]{:S(2)}, u32[]{:S(2)}) collective-permute-start(bf16[96,512]{1,0:T(8,128)(2,1)S(1)} %broadcast_select_fusion.4.refs_2_), channel_id=1, source_target_pairs={{0,4},{4,0},{8,12},{12,8},{16,20},{20,16},{24,28},{28,24},{1,5},{5... | collective-permute-start | bytes 294920 | tf_op jit(solution)/shard_map/ppermute | solution.py:154
  30.0 9.2 %collective-permute-start.7 = (bf16[96,512]{1,0:T(8,128)(2,1)S(1)}, bf16[96,512]{1,0:T(8,128)(2,1)S(1)}, u32[]{:S(2)}, u32[]{:S(2)}) collective-permute-start(bf16[96,512]{1,0:T(8,128)(2,1)S(1)} %broadcast_select_fusion.1.refs_3_), channel_id=1, source_target_pairs={{0,4},{4,0},{8,12},{12,8},{16,20},{20,16},{24,28},{28,24},{1,5},{5... | collective-permute-start | bytes 294920 | tf_op jit(solution)/shard_map/ppermute | solution.py:154

commit v2 on v0

--- a/solution.py
+++ b/solution.py
@@ -19,8 +19,13 @@
     return (widened * scale).astype(jnp.bfloat16)
 
 
-def place_kernel(groups, capacity, parts, place_ref, points_ref, assignment_ref, panel_ref, *outs):
-    points_out, tags_out, mine_out, other_out = outs
+def pick_kernel(keep_ref, *refs):
+    outs = refs[-(len(refs) // 3) :]
+    for at, out in enumerate(outs):
+        out[...] = jnp.where(keep_ref[at] != 0, refs[2 * at][...], refs[2 * at + 1][...])
+
+
+def place_kernel(groups, capacity, points_ref, assignment_ref, after_ref, points_out, tags_out):
     point_rows = points_ref.shape[0]
     ids = assignment_ref[...]
     owned = CLUSTERS // groups
@@ -54,22 +59,16 @@
         NT,
         preferred_element_type=jnp.float32,
     ).astype(jnp.bfloat16)
-    half = panel_ref.shape[1] // parts // 2
-    core = lax.rem(place_ref[0], 2)
-    for part in range(parts):
-        first = part * (2 * half)
-        for out, side in ((mine_out, core), (other_out, 1 - core)):
-            out[part * half : (part + 1) * half, :] = panel_ref[
-                0, pl.ds(pl.multiple_of(first + side * half, 16), half), :
-            ]
-
-
-def rows_kernel(groups, capacity, points_ref, partner_ref, tags_ref, halves_ref, out_ref, marks_ref):
-    half, marks = halves_ref.shape[1], marks_ref.shape[0]
+
+
+def rows_kernel(groups, capacity, place_ref, points_ref, partner_ref, tags_ref, *refs):
+    halves, out_ref, marks_ref = refs[:-2], refs[-2], refs[-1]
+    half, marks = halves[0].shape[0], marks_ref.shape[0]
     slots = points_ref.shape[0]
     tag_lanes = tags_ref.shape[1]
-    for part in range(halves_ref.shape[0]):
-        marks_ref[part * half : (part + 1) * half, :] = unit_rows(halves_ref[part])
+    for away, block in enumerate(halves):
+        first = pl.multiple_of(lax.bitwise_xor(place_ref[0], away) * half, 16)
+        marks_ref[pl.ds(first, half), :] = unit_rows(block[...])
     for core, (placed, tags) in enumerate(
         ((points_ref, tags_ref[...]), (partner_ref, jnp.zeros((slots, tag_lanes), jnp.bfloat16)))
     ):
@@ -116,18 +115,20 @@
     )[:1].astype(jnp.int32)
 
 
-def call(kernel, shapes, *operands, place=None, scratch=()):
-    whole = pl.BlockSpec(memory_space=pltpu.VMEM)
-    many = isinstance(shapes, tuple)
-    scalar = [] if place is None else [place]
+def call(kernel, shapes, *operands, place=None, after=None, scratch=()):
+    held, loose = pl.BlockSpec(memory_space=pltpu.VMEM), pl.BlockSpec(memory_space=pl.ANY)
+    first = [] if place is None else [place]
+    last = [] if after is None else [after]
     return pl.pallas_call(
         kernel,
         out_shape=shapes,
-        in_specs=[pl.BlockSpec(memory_space=pltpu.SMEM)] * len(scalar) + [whole] * len(operands),
-        out_specs=(whole,) * len(shapes) if many else whole,
+        in_specs=[pl.BlockSpec(memory_space=pltpu.SMEM)] * len(first)
+        + [held] * len(operands)
+        + [loose] * len(last),
+        out_specs=(held,) * len(shapes) if isinstance(shapes, tuple) else held,
         scratch_shapes=scratch,
         compiler_params=pltpu.CompilerParams(vmem_limit_bytes=VMEM_LIMIT),
-    )(*scalar, *operands)
+    )(*first, *operands, *last)
 
 
 def array(shape, dtype=jnp.bfloat16):
@@ -138,27 +139,30 @@
     return lax.ppermute(block, axis, [(i, i ^ mask) for i in range(lax.axis_size(axis))])
 
 
-def gather(block, axis):
-    size = lax.axis_size(axis)
-    return lax.all_to_all(
-        jnp.broadcast_to(block[None], (size,) + block.shape), axis, split_axis=0, concat_axis=0, tiled=True
-    )
-
-
-def spread(mine, other, holder, groups):
+def spread(panel, parts, holder, groups):
     me = lax.axis_index("pts")
-
-    def pick(block, mask):
-        return jnp.where(((holder ^ me) & mask) == 0, block, swap(block, "pts", mask))
-
+    sides = panel.reshape(parts, 2, -1, panel.shape[1])
+    mine, other = (
+        lax.dynamic_index_in_dim(sides, side, 1, keepdims=False).reshape(-1, panel.shape[1])
+        for side in (me % 2, 1 - me % 2)
+    )
     mine = jnp.where(((holder ^ me) & 1) == 0, mine, swap(other, "pts", 1))
     masks = [1 << bit for bit in range(1, groups.bit_length() - 1)]
     size = mine.shape[0] // len(masks)
-    blocks = [mine[at * size : (at + 1) * size] for at in range(len(masks))]
-    for turn in range(len(masks)):
-        blocks = [
-            pick(block, masks[(at + turn) % len(masks)]) for at, block in enumerate(blocks)
-        ]
+    pairs = []
+    for at, mask in enumerate(masks):
+        block = mine[at * size : (at + 1) * size]
+        pairs += [block, swap(block, "pts", mask)]
+    keep = jnp.stack([((holder ^ me) & mask) == 0 for mask in masks]).astype(jnp.int32)
+    return masks, pairs, keep
+
+
+def spread_on(blocks, masks, holder):
+    me = lax.axis_index("pts")
+    for turn in range(1, len(masks)):
+        for at, block in enumerate(blocks):
+            mask = masks[(at + turn) % len(masks)]
+            blocks[at] = jnp.where(((holder ^ me) & mask) == 0, block, swap(block, "pts", mask))
     return blocks + [swap(block, "pts", 1) for block in blocks]
 
 
@@ -185,33 +189,30 @@
     depth, columns = panels.shape[1:]
     half = landmarks.shape[0] // 2
     lanes = -(-(depth // 2 + 2) // LANES) * LANES
-    place = jnp.stack([lax.axis_index("pts"), lax.axis_index("lmk")]).astype(jnp.int32)
-    mine = lax.dynamic_slice_in_dim(landmarks, (place[0] % 2) * half, half, 0)
-    halves = gather(mine, "lmk")
-    placed, tags, panel_mine, panel_other = call(
-        lambda *refs: place_kernel(groups, capacity, parts, *refs),
-        (
-            array((slots, width)),
-            array((slots, lanes - depth // 2)),
-            array((depth // 2, columns)),
-            array((depth // 2, columns)),
-        ),
+    line = lax.axis_index("lmk").astype(jnp.int32).reshape(1)
+    mine = lax.dynamic_slice_in_dim(landmarks, (lax.axis_index("pts") % 2) * half, half, 0)
+    halves = [mine] + [swap(mine, "lmk", mask) for mask in range(1, parts)]
+    masks, pairs, keep = spread(panels[0], parts, panel_index[0], groups)
+    placed, tags = call(
+        lambda *refs: place_kernel(groups, capacity, *refs),
+        (array((slots, width)), array((slots, lanes - depth // 2))),
         points,
         assignment.reshape(1, point_rows),
-        panels,
-        place=place,
+        after=pairs[0],
     )
     partner = swap(placed, "pts", 1)
-    blocks = spread(panel_mine, panel_other, panel_index[0], groups)
     rows = call(
         lambda *refs: rows_kernel(groups, capacity, *refs),
         array((groups, 2, capacity, lanes) if capacity % 16 == 0 else (2, slots, lanes)),
         placed,
         partner,
         tags,
-        halves,
+        *halves,
+        place=line,
         scratch=[pltpu.VMEM((depth // 2, width), jnp.bfloat16)],
     )
+    blocks = call(pick_kernel, (array(pairs[0].shape),) * len(masks), *pairs, place=keep, after=rows)
+    blocks = spread_on(list(blocks), masks, panel_index[0])
     even, odd = exchange(rows, groups, capacity)
     totals, counts = call(
         lambda *refs: sums_kernel(CLUSTERS / (point_rows * groups), *refs),

time: 39.3 us -> 37.8 us (0.962)
  local copies, waits for them, and re-layouts: 3.49 us -> 2.1 us
  starting transfers between devices: 16.2 us -> 16.8 us
  waiting for transfers between devices: 13.1 us -> 12.5 us
    ppermute x8 -> x11, starting transfers between devices: 6.55 us -> 13.3 us  [swap(): lax.ppermute(block, axis, [(i, i ^ mask) for i in range(lax.axis_size(axi...]
    all_to_all x1 -> x0, starting transfers between devices: 5.91 us -> none  [gather(): lax.all_to_all(jnp.broadcast_to(block[None], (size,) + block.shape), axis...]
    unnamed x8 -> x6, local copies, waits for them, and re-layouts: 2.68 us -> 0.94 us
    dynamic_slice x1 -> x2, local copies, waits for them, and re-layouts: 0.01 us -> 1.1 us  [the longest x1 1.09 us: spread(): lax.dynamic_index_in_dim(sides, side, 1, keepdims=False)]
    all_to_all x1 -> x0, waiting for transfers between devices: 0.84 us -> none  [gather(): lax.all_to_all(jnp.broadcast_to(block[None], (size,) + block.shape), axis...]
    broadcast_in_dim x1 -> x0, local copies, waits for them, and re-layouts: 0.73 us -> none  [gather(): jnp.broadcast_to(block[None], (size,) + block.shape)]
    ppermute x8 -> x11, waiting for transfers between devices: 3.24 us -> 3.51 us  [swap(): lax.ppermute(block, axis, [(i, i ^ mask) for i in range(lax.axis_size(axi...]
    pallas_call x3 -> x4, Pallas kernels: 4.55 us -> 4.63 us  [call(): pl.pallas_call(kernel, out_shape=shapes, in_specs=[pl.BlockSpec(memory_sp...]
  transfers between devices with their start and end apart: 10 -> 12, of which waited for: 4 -> 3; matrix products, arithmetic and copies ran while one was open for 2% -> 0% of each run, Pallas kernels for 4% -> 4%
where the time goes in v2:
time: 37.8 us; the launch traced here: 37.6 us
  starting transfers between devices  16.8 us (44%)
  waiting for transfers between devices  12.5 us (33%)
  Pallas kernels  4.63 us (12%)
  local copies, waits for them, and re-layouts  2.1 us (6%)
  between operations  1.43 us (4%)
    ppermute x11, starting transfers between devices, swap(): lax.ppermute(block, axis, [(i, i ^ mask) for i in range(lax.axis_size(axi...  13.3 us
    all_to_all x1, waiting for transfers between devices, exchange(): lax.all_to_all(rows.reshape(groups, 2 * capacity, lanes), 'pts', split_ax...  8.98 us
    pallas_call x4, Pallas kernels, call(): pl.pallas_call(kernel, out_shape=shapes, in_specs=[pl.BlockSpec(memory_sp...  4.63 us
    ppermute x11, waiting for transfers between devices, swap(): lax.ppermute(block, axis, [(i, i ^ mask) for i in range(lax.axis_size(axi...  3.51 us
    all_to_all x1, starting transfers between devices, exchange(): lax.all_to_all(rows.reshape(groups, 2 * capacity, lanes), 'pts', split_ax...  3.49 us
    dynamic_slice x1, local copies, waits for them, and re-layouts, spread(): lax.dynamic_index_in_dim(sides, side, 1, keepdims=False)  1.09 us
    unnamed x6, local copies, waits for them, and re-layouts  0.94 us
  transfers between devices with their start and end apart: 12, of which 3 were waited for; matrix products, arithmetic and copies ran while one was open for 0% of the time, Pallas kernels for 4%

profile of v2, /device:TPU:0, one launch (start us, length us, event | category | flops | bytes accessed | tf_op | source)
XLA Modules:
  0.0 37.6 jit_solution(13952232037719546417)
XLA Ops:
  0.6 0.0 copy-start
  0.7 1.1 %constant_dynamic-slice_fusion.3 = (bf16[4,1,48,512]{3,2,1,0:T(8,128)(2,1)S(1)}, bf16[4,1,48,512]{3,2,1,0:T(8,128)(2,1)S(1)}) fusion(bf16[4,2,48,512]{3,2,1,0:T(8,128)(2,1)} %bitcast.25, s32[]{:T(128)S(6)} %select_n.50, s32[]{:T(128)S(6)} %select_n.51), kind=kLoop, calls=%fused_computation.9 | loop fusion | bytes 786440 | tf_op jit(solution)/shard_map/jit(dynamic_index_in_dim)/dynamic_slice | solution.py:146
  1.8 0.5 %collective-permute-start = (bf16[192,512]{1,0:T(8,128)(2,1)S(1)}, bf16[192,512]{1,0:T(8,128)(2,1)S(1)}, u32[]{:S(2)}, u32[]{:S(2)}) collective-permute-start(bf16[192,512]{1,0:T(8,128)(2,1)S(1)} %bitcast.26), channel_id=1, source_target_pairs={{0,4},{4,0},{8,12},{12,8},{16,20},{20,16},{24,28},{28,24},{1,5},{5... | collective-permute-start | bytes 589832 | tf_op jit(solution)/shard_map/ppermute | solution.py:139
  2.9 0.4 %collective-permute-done = bf16[192,512]{1,0:T(8,128)(2,1)S(1)} collective-permute-done((bf16[192,512]{1,0:T(8,128)(2,1)S(1)}, bf16[192,512]{1,0:T(8,128)(2,1)S(1)}, u32[]{:S(2)}, u32[]{:S(2)}) %collective-permute-start) | collective-permute-done | bytes 196640 | tf_op jit(solution)/shard_map/ppermute | solution.py:139
  3.4 0.0 copy-start.2
  3.4 0.9 %copy-done.1 = bf16[256,768]{1,0:T(8,128)(2,1)S(1)} copy-done((bf16[256,768]{1,0:T(8,128)(2,1)S(1)}, bf16[256,768]{1,0:T(8,128)(2,1)}, u32[]{:S(2)}) %copy-start.1) | copy-done | bytes 393240
  4.4 0.6 %shard_map.68 = (bf16[512,768]{1,0:T(8,128)(2,1)S(1)}, bf16[512,64]{1,0:T(8,128)(2,1)S(1)}) custom-call(bf16[256,768]{1,0:T(8,128)(2,1)S(1)} %copy-done.1, s32[1,256]{1,0:T(1,128)S(1)} %bitcast.23, bf16[96,512]{1,0:T(8,128)(2,1)S(1)} %get-tuple-element.21.refs_2_.refs_0_), custom_call_target="tpu_custom_call" | custom-call | tf_op jit(solution)/shard_map/pallas_call | solution.py:122
  5.0 0.4 %collective-permute-start.1 = (bf16[512,768]{1,0:T(8,128)(2,1)S(1)}, bf16[512,768]{1,0:T(8,128)(2,1)S(1)}, u32[]{:S(2)}, u32[]{:S(2)}) collective-permute-start(bf16[512,768]{1,0:T(8,128)(2,1)S(1)} %get-tuple-element.8.refs_1_), channel_id=1, source_target_pairs={{0,4},{4,0},{8,12},{12,8},{16,20},{20,16},{24,28},{28,24},{1,5},{5... | collective-permute-start | bytes 2359304 | tf_op jit(solution)/shard_map/ppermute | solution.py:139
  5.4 2.8 %collective-permute-start.2 = (bf16[48,768]{1,0:T(8,128)(2,1)S(1)}, bf16[48,768]{1,0:T(8,128)(2,1)S(1)}, u32[]{:S(2)}, u32[]{:S(2)}) collective-permute-start(bf16[48,768]{1,0:T(8,128)(2,1)S(1)} %constant_dynamic-slice_fusion.1.refs_4_), channel_id=1, source_target_pairs={{0,1},{1,0},{2,3},{3,2},{4,5},{5,4},{6,7},{7,6},{8,9},{9,8},{10,11... | collective-permute-start | bytes 221192 | tf_op jit(solution)/shard_map/ppermute | solution.py:139
  8.2 2.6 %collective-permute-start.3 = (bf16[48,768]{1,0:T(8,128)(2,1)S(1)}, bf16[48,768]{1,0:T(8,128)(2,1)S(1)}, u32[]{:S(2)}, u32[]{:S(2)}) collective-permute-start(bf16[48,768]{1,0:T(8,128)(2,1)S(1)} %constant_dynamic-slice_fusion.1.refs_4_), channel_id=1, source_target_pairs={{0,2},{1,3},{2,0},{3,1},{4,6},{5,7},{6,4},{7,5},{8,10},{9,11},{10,... | collective-permute-start | bytes 221192 | tf_op jit(solution)/shard_map/ppermute | solution.py:139
  10.8 1.7 %collective-permute-start.5 = (bf16[96,512]{1,0:T(8,128)(2,1)S(1)}, bf16[96,512]{1,0:T(8,128)(2,1)S(1)}, u32[]{:S(2)}, u32[]{:S(2)}) collective-permute-start(bf16[96,512]{1,0:T(8,128)(2,1)S(1)} %get-tuple-element.21.refs_2_.refs_0_), channel_id=1, source_target_pairs={{0,8},{4,12},{8,0},{12,4},{16,24},{20,28},{24,16},{28,20},{1,9},{5... | collective-permute-start | bytes 294920 | tf_op jit(solution)/shard_map/ppermute | solution.py:139
  12.5 1.5 %collective-permute-start.6 = (bf16[96,512]{1,0:T(8,128)(2,1)S(1)}, bf16[96,512]{1,0:T(8,128)(2,1)S(1)}, u32[]{:S(2)}, u32[]{:S(2)}) collective-permute-start(bf16[96,512]{1,0:T(8,128)(2,1)S(1)} %get-tuple-element.20.refs_2_), channel_id=1, source_target_pairs={{0,16},{4,20},{8,24},{12,28},{16,0},{20,4},{24,8},{28,12},{1,17},{... | collective-permute-start | bytes 294920 | tf_op jit(solution)/shard_map/ppermute | solution.py:139
  14.0 0.1 add_convert_fusion.keep_ref
  14.1 3.1 %collective-permute-done.3.refs_6_ = bf16[48,768]{1,0:T(8,128)(2,1)S(1)} collective-permute-done((bf16[48,768]{1,0:T(8,128)(2,1)S(1)}, bf16[48,768]{1,0:T(8,128)(2,1)S(1)}, u32[]{:S(2)}, u32[]{:S(2)}) %collective-permute-start.3) | collective-permute-done | bytes 73760 | tf_op jit(solution)/shard_map/ppermute | solution.py:139
  17.2 0.0 collective-permute-done.4.refs_7_
  17.2 1.6 %shard_map.69.refs_4_ = bf16[8,2,64,256]{3,2,1,0:T(8,128)(2,1)} custom-call(s32[1]{0:T(128)} %bitcast.refs_0_, bf16[512,768]{1,0:T(8,128)(2,1)S(1)} %get-tuple-element.8.refs_1_, bf16[512,768]{1,0:T(8,128)(2,1)S(1)} %collective-permute-done.1.refs_2_, bf16[512,64]{1,0:T(8,128)(2,1)S(1)} %get-tuple-element.9.refs_3_, ...), custom_call_target="tpu_custom_call" | custom-call | tf_op jit(solution)/shard_map/pallas_call | solution.py:122
  18.8 0.6 %shard_map.70 = (bf16[96,512]{1,0:T(8,128)(2,1)S(1)}, bf16[96,512]{1,0:T(8,128)(2,1)S(1)}) custom-call(s32[2]{0:T(128)S(1)} %add_convert_fusion.keep_ref, bf16[96,512]{1,0:T(8,128)(2,1)S(1)} %get-tuple-element.21.refs_2_.refs_0_, bf16[96,512]{1,0:T(8,128)(2,1)S(1)} %collective-permute-done.5.refs_1_, bf16[96,512]{1,0:T(8,128)(2,1)S(1)} %get-tuple-element.20.refs_2_, ...), custom_call_target="tpu_custom_call" | custom-call | tf_op jit(solution)/shard_map/pallas_call | solution.py:122
  19.3 1.6 %collective-permute-start.8 = (bf16[96,512]{1,0:T(8,128)(2,1)S(1)}, bf16[96,512]{1,0:T(8,128)(2,1)S(1)}, u32[]{:S(2)}, u32[]{:S(2)}) collective-permute-start(bf16[96,512]{1,0:T(8,128)(2,1)S(1)} %get-tuple-element.11), channel_id=1, source_target_pairs={{0,8},{4,12},{8,0},{12,4},{16,24},{20,28},{24,16},{28,20},{1,9},{5... | collective-permute-start | bytes 294920 | tf_op jit(solution)/shard_map/ppermute | solution.py:139
  20.9 1.5 %collective-permute-start.7 = (bf16[96,512]{1,0:T(8,128)(2,1)S(1)}, bf16[96,512]{1,0:T(8,128)(2,1)S(1)}, u32[]{:S(2)}, u32[]{:S(2)}) collective-permute-start(bf16[96,512]{1,0:T(8,128)(2,1)S(1)} %get-tuple-element.10), channel_id=1, source_target_pairs={{0,16},{4,20},{8,24},{12,28},{16,0},{20,4},{24,8},{28,12},{1,17},{... | collective-permute-start | bytes 294920 | tf_op jit(solution)/shard_map/ppermute | solution.py:139
  22.4 3.5 %all-to-all-start = ((bf16[8,128,256]{2,1,0:T(8,128)(2,1)}), bf16[8,128,256]{2,1,0:T(8,128)(2,1)S(1)}, u32[]{:S(2)}, u32[]{:S(2)}) async-start(bf16[8,128,256]{2,1,0:T(8,128)(2,1)} %bitcast.6), calls=%async_computation | async-start | bytes 1048576 | tf_op jit(solution)/shard_map/all_to_all | solution.py:173
  25.9 0.5 %collective-permute-start.10 = (bf16[96,512]{1,0:T(8,128)(2,1)S(1)}, bf16[96,512]{1,0:T(8,128)(2,1)S(1)}, u32[]{:S(2)}, u32[]{:S(2)}) collective-permute-start(bf16[96,512]{1,0:T(8,128)(2,1)S(1)} %broadcast_select_fusion.refs_3_), channel_id=1, source_target_pairs={{0,4},{4,0},{8,12},{12,8},{16,20},{20,16},{24,28},{28,24},{1,5},{5... | collective-permute-start | bytes 294920 | tf_op jit(solution)/shard_map/ppermute | solution.py:139
  26.4 0.2 collective-permute-start.9
  26.6 9.0 %all-to-all-done = bf16[8,128,256]{2,1,0:T(8,128)(2,1)S(1)} async-done(((bf16[8,128,256]{2,1,0:T(8,128)(2,1)}), bf16[8,128,256]{2,1,0:T(8,128)(2,1)S(1)}, u32[]{:S(2)}, u32[]{:S(2)}) %all-to-all-start) | async-done | bytes 524320 | tf_op jit(solution)/shard_map/all_to_all | solution.py:173
  35.7 1.9 %shard_map.71 = (f32[512,512]{1,0:T(8,128)}, s32[1,512]{1,0:T(1,128)}) custom-call(bf16[512,256]{1,0:T(8,128)(2,1)S(1)} %bitcast.21, bf16[512,256]{1,0:T(8,128)(2,1)S(1)} %bitcast.22, bf16[96,512]{1,0:T(8,128)(2,1)S(1)} %broadcast_select_fusion.1.refs_2_, bf16[96,512]{1,0:T(8,128)(2,1)S(1)} %broadcast_select_fusion.refs_3_, ...), custom_call_target="tpu_custom_call" | custom-call | tf_op jit(solution)/shard_map/pallas_call | solution.py:122
  (20 shorter events, 0.2 us)
Async XLA Ops:
  0.6 4.8 %copy-start = (bf16[96,768]{1,0:T(8,128)(2,1)S(1)}, bf16[96,768]{1,0:T(8,128)(2,1)}, u32[]{:S(2)}) copy-start(bf16[96,768]{1,0:T(8,128)(2,1)} %param.6) | copy-start | bytes 442372
  1.8 1.6 %collective-permute-start = (bf16[192,512]{1,0:T(8,128)(2,1)S(1)}, bf16[192,512]{1,0:T(8,128)(2,1)S(1)}, u32[]{:S(2)}, u32[]{:S(2)}) collective-permute-start(bf16[192,512]{1,0:T(8,128)(2,1)S(1)} %bitcast.26), channel_id=1, source_target_pairs={{0,4},{4,0},{8,12},{12,8},{16,20},{20,16},{24,28},{28,24},{1,5},{5... | collective-permute-start | bytes 589832 | tf_op jit(solution)/shard_map/ppermute | solution.py:139
  3.4 1.0 %copy-start.1 = (bf16[256,768]{1,0:T(8,128)(2,1)S(1)}, bf16[256,768]{1,0:T(8,128)(2,1)}, u32[]{:S(2)}) copy-start(bf16[256,768]{1,0:T(8,128)(2,1)} %refs_0_.1) | copy-start | bytes 1179652
  3.4 0.9 %copy-start.2 = (s32[256]{0:T(256)S(1)}, s32[256]{0:T(256)}, u32[]{:S(2)}) copy-start(s32[256]{0:T(256)} %param.9) | copy-start | bytes 3076
  5.0 12.2 %collective-permute-start.1 = (bf16[512,768]{1,0:T(8,128)(2,1)S(1)}, bf16[512,768]{1,0:T(8,128)(2,1)S(1)}, u32[]{:S(2)}, u32[]{:S(2)}) collective-permute-start(bf16[512,768]{1,0:T(8,128)(2,1)S(1)} %get-tuple-element.8.refs_1_), channel_id=1, source_target_pairs={{0,4},{4,0},{8,12},{12,8},{16,20},{20,16},{24,28},{28,24},{1,5},{5... | collective-permute-start | bytes 2359304 | tf_op jit(solution)/shard_map/ppermute | solution.py:139
  5.4 7.1 %collective-permute-start.2 = (bf16[48,768]{1,0:T(8,128)(2,1)S(1)}, bf16[48,768]{1,0:T(8,128)(2,1)S(1)}, u32[]{:S(2)}, u32[]{:S(2)}) collective-permute-start(bf16[48,768]{1,0:T(8,128)(2,1)S(1)} %constant_dynamic-slice_fusion.1.refs_4_), channel_id=1, source_target_pairs={{0,1},{1,0},{2,3},{3,2},{4,5},{5,4},{6,7},{7,6},{8,9},{9,8},{10,11... | collective-permute-start | bytes 221192 | tf_op jit(solution)/shard_map/ppermute | solution.py:139
  8.2 9.0 %collective-permute-start.3 = (bf16[48,768]{1,0:T(8,128)(2,1)S(1)}, bf16[48,768]{1,0:T(8,128)(2,1)S(1)}, u32[]{:S(2)}, u32[]{:S(2)}) collective-permute-start(bf16[48,768]{1,0:T(8,128)(2,1)S(1)} %constant_dynamic-slice_fusion.1.refs_4_), channel_id=1, source_target_pairs={{0,2},{1,3},{2,0},{3,1},{4,6},{5,7},{6,4},{7,5},{8,10},{9,11},{10,... | collective-permute-start | bytes 221192 | tf_op jit(solution)/shard_map/ppermute | solution.py:139
  10.8 6.4 %collective-permute-start.4 = (bf16[48,768]{1,0:T(8,128)(2,1)S(1)}, bf16[48,768]{1,0:T(8,128)(2,1)S(1)}, u32[]{:S(2)}, u32[]{:S(2)}) collective-permute-start(bf16[48,768]{1,0:T(8,128)(2,1)S(1)} %constant_dynamic-slice_fusion.1.refs_4_), channel_id=1, source_target_pairs={{0,3},{1,2},{2,1},{3,0},{4,7},{5,6},{6,5},{7,4},{8,11},{9,10},{10,... | collective-permute-start | bytes 221192 | tf_op jit(solution)/shard_map/ppermute | solution.py:139
  10.8 7.9 %collective-permute-start.5 = (bf16[96,512]{1,0:T(8,128)(2,1)S(1)}, bf16[96,512]{1,0:T(8,128)(2,1)S(1)}, u32[]{:S(2)}, u32[]{:S(2)}) collective-permute-start(bf16[96,512]{1,0:T(8,128)(2,1)S(1)} %get-tuple-element.21.refs_2_.refs_0_), channel_id=1, source_target_pairs={{0,8},{4,12},{8,0},{12,4},{16,24},{20,28},{24,16},{28,20},{1,9},{5... | collective-permute-start | bytes 294920 | tf_op jit(solution)/shard_map/ppermute | solution.py:139
  12.5 6.2 %collective-permute-start.6 = (bf16[96,512]{1,0:T(8,128)(2,1)S(1)}, bf16[96,512]{1,0:T(8,128)(2,1)S(1)}, u32[]{:S(2)}, u32[]{:S(2)}) collective-permute-start(bf16[96,512]{1,0:T(8,128)(2,1)S(1)} %get-tuple-element.20.refs_2_), channel_id=1, source_target_pairs={{0,16},{4,20},{8,24},{12,28},{16,0},{20,4},{24,8},{28,12},{1,17},{... | collective-permute-start | bytes 294920 | tf_op jit(solution)/shard_map/ppermute | solution.py:139
  19.3 6.6 %collective-permute-start.8 = (bf16[96,512]{1,0:T(8,128)(2,1)S(1)}, bf16[96,512]{1,0:T(8,128)(2,1)S(1)}, u32[]{:S(2)}, u32[]{:S(2)}) collective-permute-start(bf16[96,512]{1,0:T(8,128)(2,1)S(1)} %get-tuple-element.11), channel_id=1, source_target_pairs={{0,8},{4,12},{8,0},{12,4},{16,24},{20,28},{24,16},{28,20},{1,9},{5... | collective-permute-start | bytes 294920 | tf_op jit(solution)/shard_map/ppermute | solution.py:139
  20.9 5.5 %collective-permute-start.7 = (bf16[96,512]{1,0:T(8,128)(2,1)S(1)}, bf16[96,512]{1,0:T(8,128)(2,1)S(1)}, u32[]{:S(2)}, u32[]{:S(2)}) collective-permute-start(bf16[96,512]{1,0:T(8,128)(2,1)S(1)} %get-tuple-element.10), channel_id=1, source_target_pairs={{0,16},{4,20},{8,24},{12,28},{16,0},{20,4},{24,8},{28,12},{1,17},{... | collective-permute-start | bytes 294920 | tf_op jit(solution)/shard_map/ppermute | solution.py:139
  22.4 13.2 %all-to-all-start = ((bf16[8,128,256]{2,1,0:T(8,128)(2,1)}), bf16[8,128,256]{2,1,0:T(8,128)(2,1)S(1)}, u32[]{:S(2)}, u32[]{:S(2)}) async-start(bf16[8,128,256]{2,1,0:T(8,128)(2,1)} %bitcast.6), calls=%async_computation | async-start | bytes 1048576 | tf_op jit(solution)/shard_map/all_to_all | solution.py:173
  25.9 9.7 %collective-permute-start.10 = (bf16[96,512]{1,0:T(8,128)(2,1)S(1)}, bf16[96,512]{1,0:T(8,128)(2,1)S(1)}, u32[]{:S(2)}, u32[]{:S(2)}) collective-permute-start(bf16[96,512]{1,0:T(8,128)(2,1)S(1)} %broadcast_select_fusion.refs_3_), channel_id=1, source_target_pairs={{0,4},{4,0},{8,12},{12,8},{16,20},{20,16},{24,28},{28,24},{1,5},{5... | collective-permute-start | bytes 294920 | tf_op jit(solution)/shard_map/ppermute | solution.py:139
  26.4 9.3 %collective-permute-start.9 = (bf16[96,512]{1,0:T(8,128)(2,1)S(1)}, bf16[96,512]{1,0:T(8,128)(2,1)S(1)}, u32[]{:S(2)}, u32[]{:S(2)}) collective-permute-start(bf16[96,512]{1,0:T(8,128)(2,1)S(1)} %broadcast_select_fusion.1.refs_2_), channel_id=1, source_target_pairs={{0,4},{4,0},{8,12},{12,8},{16,20},{20,16},{24,28},{28,24},{1,5},{5... | collective-permute-start | bytes 294920 | tf_op jit(solution)/shard_map/ppermute | solution.py:139

commit v3 on v2

--- a/solution.py
+++ b/solution.py
@@ -19,61 +19,58 @@
     return (widened * scale).astype(jnp.bfloat16)
 
 
-def pick_kernel(keep_ref, *refs):
-    outs = refs[-(len(refs) // 3) :]
-    for at, out in enumerate(outs):
-        out[...] = jnp.where(keep_ref[at] != 0, refs[2 * at][...], refs[2 * at + 1][...])
-
-
-def place_kernel(groups, capacity, points_ref, assignment_ref, after_ref, points_out, tags_out):
-    point_rows = points_ref.shape[0]
-    ids = assignment_ref[...]
-    owned = CLUSTERS // groups
-    owners = lax.div(ids, owned)
-    tags = ids - owners * owned + 1
-    hits = lax.broadcasted_iota(jnp.int32, (groups, point_rows), 0) == owners
-    earlier = lax.broadcasted_iota(jnp.int32, (point_rows, point_rows), 0) < lax.broadcasted_iota(
-        jnp.int32, (point_rows, point_rows), 1
-    )
-    before = jnp.dot(
-        hits.astype(jnp.float32).astype(jnp.bfloat16),
-        earlier.astype(jnp.float32).astype(jnp.bfloat16),
-        preferred_element_type=jnp.float32,
-    )
-    rank = jnp.sum(jnp.where(hits, before, 0.0), axis=0, keepdims=True).astype(jnp.int32)
-    slots = owners * capacity + rank
-    placed = (
-        (lax.broadcasted_iota(jnp.int32, (groups * capacity, point_rows), 0) == slots)
-        .astype(jnp.float32)
-        .astype(jnp.bfloat16)
-    )
-    points_out[...] = jnp.dot(
-        placed, unit_rows(points_ref[...]), preferred_element_type=jnp.float32
-    ).astype(jnp.bfloat16)
-    high = lax.div(tags, 256)
-    which = lax.broadcasted_iota(jnp.int32, (tags_out.shape[1], point_rows), 0)
-    coded = jnp.where(which == 0, high, jnp.where(which == 1, tags - high * 256, 0))
-    tags_out[...] = lax.dot_general(
-        placed,
-        coded.astype(jnp.float32).astype(jnp.bfloat16),
-        NT,
-        preferred_element_type=jnp.float32,
-    ).astype(jnp.bfloat16)
-
-
-def rows_kernel(groups, capacity, place_ref, points_ref, partner_ref, tags_ref, *refs):
+def place_kernel(groups, capacity, *refs):
+    points_out, tags_out = refs[-2:]
+    for core in range(2):
+        points_ref, assignment_ref = refs[2 * core : 2 * core + 2]
+        point_rows = points_ref.shape[0]
+        ids = assignment_ref[...]
+        owned = CLUSTERS // groups
+        owners = lax.div(ids, owned)
+        tags = ids - owners * owned + 1
+        hits = lax.broadcasted_iota(jnp.int32, (groups, point_rows), 0) == owners
+        earlier = lax.broadcasted_iota(
+            jnp.int32, (point_rows, point_rows), 0
+        ) < lax.broadcasted_iota(jnp.int32, (point_rows, point_rows), 1)
+        before = jnp.dot(
+            hits.astype(jnp.float32).astype(jnp.bfloat16),
+            earlier.astype(jnp.float32).astype(jnp.bfloat16),
+            preferred_element_type=jnp.float32,
+        )
+        rank = jnp.sum(jnp.where(hits, before, 0.0), axis=0, keepdims=True).astype(jnp.int32)
+        slots = owners * capacity + rank
+        placed = (
+            (lax.broadcasted_iota(jnp.int32, (groups * capacity, point_rows), 0) == slots)
+            .astype(jnp.float32)
+            .astype(jnp.bfloat16)
+        )
+        points_out[core] = jnp.dot(
+            placed, unit_rows(points_ref[...]), preferred_element_type=jnp.float32
+        ).astype(jnp.bfloat16)
+        if core == 0:
+            high = lax.div(tags, 256)
+            which = lax.broadcasted_iota(jnp.int32, (tags_out.shape[1], point_rows), 0)
+            coded = jnp.where(which == 0, high, jnp.where(which == 1, tags - high * 256, 0))
+            tags_out[...] = lax.dot_general(
+                placed,
+                coded.astype(jnp.float32).astype(jnp.bfloat16),
+                NT,
+                preferred_element_type=jnp.float32,
+            ).astype(jnp.bfloat16)
+
+
+def rows_kernel(groups, capacity, place_ref, points_ref, tags_ref, *refs):
     halves, out_ref, marks_ref = refs[:-2], refs[-2], refs[-1]
     half, marks = halves[0].shape[0], marks_ref.shape[0]
-    slots = points_ref.shape[0]
-    tag_lanes = tags_ref.shape[1]
+    no_tags = jnp.zeros(tags_ref.shape, jnp.bfloat16)
     for away, block in enumerate(halves):
         first = pl.multiple_of(lax.bitwise_xor(place_ref[0], away) * half, 16)
         marks_ref[pl.ds(first, half), :] = unit_rows(block[...])
-    for core, (placed, tags) in enumerate(
-        ((points_ref, tags_ref[...]), (partner_ref, jnp.zeros((slots, tag_lanes), jnp.bfloat16)))
-    ):
-        scores = lax.dot_general(placed[...], marks_ref[...], NT, preferred_element_type=jnp.float32)
-        rows = jnp.exp(scores * (0.5 / math.sqrt(placed.shape[1]))).astype(jnp.bfloat16)
+    for core, tags in enumerate((tags_ref[...], no_tags)):
+        scores = lax.dot_general(
+            points_ref[core], marks_ref[...], NT, preferred_element_type=jnp.float32
+        )
+        rows = jnp.exp(scores * (0.5 / math.sqrt(points_ref.shape[2]))).astype(jnp.bfloat16)
         if len(out_ref.shape) == 4:
             for group in range(groups):
                 here = slice(group * capacity, (group + 1) * capacity)
@@ -115,20 +112,17 @@
     )[:1].astype(jnp.int32)
 
 
-def call(kernel, shapes, *operands, place=None, after=None, scratch=()):
-    held, loose = pl.BlockSpec(memory_space=pltpu.VMEM), pl.BlockSpec(memory_space=pl.ANY)
+def call(kernel, shapes, *operands, place=None, scratch=()):
+    held = pl.BlockSpec(memory_space=pltpu.VMEM)
     first = [] if place is None else [place]
-    last = [] if after is None else [after]
     return pl.pallas_call(
         kernel,
         out_shape=shapes,
-        in_specs=[pl.BlockSpec(memory_space=pltpu.SMEM)] * len(first)
-        + [held] * len(operands)
-        + [loose] * len(last),
+        in_specs=[pl.BlockSpec(memory_space=pltpu.SMEM)] * len(first) + [held] * len(operands),
         out_specs=(held,) * len(shapes) if isinstance(shapes, tuple) else held,
         scratch_shapes=scratch,
         compiler_params=pltpu.CompilerParams(vmem_limit_bytes=VMEM_LIMIT),
-    )(*first, *operands, *last)
+    )(*first, *operands)
 
 
 def array(shape, dtype=jnp.bfloat16):
@@ -146,23 +140,18 @@
         lax.dynamic_index_in_dim(sides, side, 1, keepdims=False).reshape(-1, panel.shape[1])
         for side in (me % 2, 1 - me % 2)
     )
+
+    def pick(block, mask):
+        return jnp.where(((holder ^ me) & mask) == 0, block, swap(block, "pts", mask))
+
     mine = jnp.where(((holder ^ me) & 1) == 0, mine, swap(other, "pts", 1))
     masks = [1 << bit for bit in range(1, groups.bit_length() - 1)]
     size = mine.shape[0] // len(masks)
-    pairs = []
-    for at, mask in enumerate(masks):
-        block = mine[at * size : (at + 1) * size]
-        pairs += [block, swap(block, "pts", mask)]
-    keep = jnp.stack([((holder ^ me) & mask) == 0 for mask in masks]).astype(jnp.int32)
-    return masks, pairs, keep
-
-
-def spread_on(blocks, masks, holder):
-    me = lax.axis_index("pts")
-    for turn in range(1, len(masks)):
-        for at, block in enumerate(blocks):
-            mask = masks[(at + turn) % len(masks)]
-            blocks[at] = jnp.where(((holder ^ me) & mask) == 0, block, swap(block, "pts", mask))
+    blocks = [mine[at * size : (at + 1) * size] for at in range(len(masks))]
+    for turn in range(len(masks)):
+        blocks = [
+            pick(block, masks[(at + turn) % len(masks)]) for at, block in enumerate(blocks)
+        ]
     return blocks + [swap(block, "pts", 1) for block in blocks]
 
 
@@ -192,27 +181,25 @@
     line = lax.axis_index("lmk").astype(jnp.int32).reshape(1)
     mine = lax.dynamic_slice_in_dim(landmarks, (lax.axis_index("pts") % 2) * half, half, 0)
     halves = [mine] + [swap(mine, "lmk", mask) for mask in range(1, parts)]
-    masks, pairs, keep = spread(panels[0], parts, panel_index[0], groups)
+    blocks = spread(panels[0], parts, panel_index[0], groups)
+    assignment = assignment.reshape(1, point_rows)
     placed, tags = call(
         lambda *refs: place_kernel(groups, capacity, *refs),
-        (array((slots, width)), array((slots, lanes - depth // 2))),
+        (array((2, slots, width)), array((slots, lanes - depth // 2))),
         points,
-        assignment.reshape(1, point_rows),
-        after=pairs[0],
-    )
-    partner = swap(placed, "pts", 1)
+        assignment,
+        swap(points, "pts", 1),
+        swap(assignment, "pts", 1),
+    )
     rows = call(
         lambda *refs: rows_kernel(groups, capacity, *refs),
         array((groups, 2, capacity, lanes) if capacity % 16 == 0 else (2, slots, lanes)),
         placed,
-        partner,
         tags,
         *halves,
         place=line,
         scratch=[pltpu.VMEM((depth // 2, width), jnp.bfloat16)],
     )
-    blocks = call(pick_kernel, (array(pairs[0].shape),) * len(masks), *pairs, place=keep, after=rows)
-    blocks = spread_on(list(blocks), masks, panel_index[0])
     even, odd = exchange(rows, groups, capacity)
     totals, counts = call(
         lambda *refs: sums_kernel(CLUSTERS / (point_rows * groups), *refs),

time: 37.8 us -> 39.3 us (1.040)
  waiting for transfers between devices: 12.5 us -> 15.4 us
  local copies, waits for them, and re-layouts: 2.1 us -> 1.2 us
  starting transfers between devices: 16.8 us -> 16.4 us
    ppermute x11 -> x12, waiting for transfers between devices: 3.51 us -> 6.34 us  [swap(): lax.ppermute(block, axis, [(i, i ^ mask) for i in range(lax.axis_size(axi...]
    unnamed x6, local copies, waits for them, and re-layouts: 0.94 us -> 0.02 us
    ppermute x11 -> x12, starting transfers between devices: 13.3 us -> 12.6 us  [swap(): lax.ppermute(block, axis, [(i, i ^ mask) for i in range(lax.axis_size(axi...]
    pallas_call x4 -> x3, Pallas kernels: 4.63 us -> 4.55 us  [call(): pl.pallas_call(kernel, out_shape=shapes, in_specs=[pl.BlockSpec(memory_sp...]
  transfers between devices with their start and end apart: 12 -> 13, of which waited for: 3 -> 6; matrix products, arithmetic and copies ran while one was open for 0% -> 0% of each run, Pallas kernels for 4% -> 7%
where the time goes in v3:
time: 39.3 us; the launch traced here: 39 us
  starting transfers between devices  16.4 us (42%)
  waiting for transfers between devices  15.4 us (39%)
  Pallas kernels  4.55 us (12%)
  between operations  1.44 us (4%)
  local copies, waits for them, and re-layouts  1.2 us (3%)
    ppermute x12, starting transfers between devices, swap(): lax.ppermute(block, axis, [(i, i ^ mask) for i in range(lax.axis_size(axi...  12.6 us
    all_to_all x1, waiting for transfers between devices, exchange(): lax.all_to_all(rows.reshape(groups, 2 * capacity, lanes), 'pts', split_ax...  9.04 us
    ppermute x12, waiting for transfers between devices, swap(): lax.ppermute(block, axis, [(i, i ^ mask) for i in range(lax.axis_size(axi...  6.34 us
    pallas_call x3, Pallas kernels, call(): pl.pallas_call(kernel, out_shape=shapes, in_specs=[pl.BlockSpec(memory_sp...  4.55 us
    all_to_all x1, starting transfers between devices, exchange(): lax.all_to_all(rows.reshape(groups, 2 * capacity, lanes), 'pts', split_ax...  3.72 us
    dynamic_slice x1, local copies, waits for them, and re-layouts, spread(): lax.dynamic_index_in_dim(sides, side, 1, keepdims=False)  1.11 us
  transfers between devices with their start and end apart: 13, of which 6 were waited for; matrix products, arithmetic and copies ran while one was open for 0% of the time, Pallas kernels for 7%

profile of v3, /device:TPU:0, one launch (start us, length us, event | category | flops | bytes accessed | tf_op | source)
XLA Modules:
  0.0 39.0 jit_solution(17296283814059726188)
XLA Ops:
  0.6 0.0 copy-start
  0.7 1.1 %constant_dynamic-slice_fusion.1 = (bf16[4,1,48,512]{3,2,1,0:T(8,128)(2,1)S(1)}, bf16[4,1,48,512]{3,2,1,0:T(8,128)(2,1)S(1)}) fusion(bf16[4,2,48,512]{3,2,1,0:T(8,128)(2,1)} %bitcast.24, s32[]{:T(128)S(6)} %select_n.58, s32[]{:T(128)S(6)} %select_n.59), kind=kLoop, calls=%fused_computation.8 | loop fusion | bytes 786440 | tf_op jit(solution)/shard_map/jit(dynamic_index_in_dim)/dynamic_slice | solution.py:140
  1.8 0.5 %collective-permute-start.5 = (bf16[192,512]{1,0:T(8,128)(2,1)S(1)}, bf16[192,512]{1,0:T(8,128)(2,1)S(1)}, u32[]{:S(2)}, u32[]{:S(2)}) collective-permute-start(bf16[192,512]{1,0:T(8,128)(2,1)S(1)} %bitcast.25), channel_id=1, source_target_pairs={{0,4},{4,0},{8,12},{12,8},{16,20},{20,16},{24,28},{28,24},{1,5},{5... | collective-permute-start | bytes 589832 | tf_op jit(solution)/shard_map/ppermute | solution.py:133
  3.0 0.4 %collective-permute-done.5 = bf16[192,512]{1,0:T(8,128)(2,1)S(1)} collective-permute-done((bf16[192,512]{1,0:T(8,128)(2,1)S(1)}, bf16[192,512]{1,0:T(8,128)(2,1)S(1)}, u32[]{:S(2)}, u32[]{:S(2)}) %collective-permute-start.5) | collective-permute-done | bytes 196640 | tf_op jit(solution)/shard_map/ppermute | solution.py:133
  3.5 3.0 %collective-permute-start.8 = (bf16[96,512]{1,0:T(8,128)(2,1)S(1)}, bf16[96,512]{1,0:T(8,128)(2,1)S(1)}, u32[]{:S(2)}, u32[]{:S(2)}) collective-permute-start(bf16[96,512]{1,0:T(8,128)(2,1)S(1)} %get-tuple-element.18), channel_id=1, source_target_pairs={{0,16},{4,20},{8,24},{12,28},{16,0},{20,4},{24,8},{28,12},{1,17},{... | collective-permute-start | bytes 294920 | tf_op jit(solution)/shard_map/ppermute | solution.py:133
  6.4 1.5 %collective-permute-start.6 = (bf16[96,512]{1,0:T(8,128)(2,1)S(1)}, bf16[96,512]{1,0:T(8,128)(2,1)S(1)}, u32[]{:S(2)}, u32[]{:S(2)}) collective-permute-start(bf16[96,512]{1,0:T(8,128)(2,1)S(1)} %get-tuple-element.19), channel_id=1, source_target_pairs={{0,8},{4,12},{8,0},{12,4},{16,24},{20,28},{24,16},{28,20},{1,9},{5... | collective-permute-start | bytes 294920 | tf_op jit(solution)/shard_map/ppermute | solution.py:133
  7.9 0.0 collective-permute-start
  7.9 0.5 %collective-permute-start.1 = (s32[1,256]{1,0:T(1,128)S(1)}, s32[1,256]{1,0:T(1,128)S(1)}, u32[]{:S(2)}, u32[]{:S(2)}) collective-permute-start(s32[1,256]{1,0:T(1,128)S(1)} %bitcast.21), channel_id=1, source_target_pairs={{0,4},{4,0},{8,12},{12,8},{16,20},{20,16},{24,28},{28,24},{1,5},{5... | collective-permute-start | bytes 3080 | tf_op jit(solution)/shard_map/ppermute | solution.py:133
  8.4 1.1 %collective-permute-done.8 = bf16[96,512]{1,0:T(8,128)(2,1)S(1)} collective-permute-done((bf16[96,512]{1,0:T(8,128)(2,1)S(1)}, bf16[96,512]{1,0:T(8,128)(2,1)S(1)}, u32[]{:S(2)}, u32[]{:S(2)}) %collective-permute-start.8) | collective-permute-done | bytes 98336 | tf_op jit(solution)/shard_map/ppermute | solution.py:133
  9.5 1.5 %collective-permute-done.6 = bf16[96,512]{1,0:T(8,128)(2,1)S(1)} collective-permute-done((bf16[96,512]{1,0:T(8,128)(2,1)S(1)}, bf16[96,512]{1,0:T(8,128)(2,1)S(1)}, u32[]{:S(2)}, u32[]{:S(2)}) %collective-permute-start.6) | collective-permute-done | bytes 98336 | tf_op jit(solution)/shard_map/ppermute | solution.py:133
  11.1 0.4 collective-permute-start.7
  11.4 1.8 %collective-permute-start.2 = (bf16[48,768]{1,0:T(8,128)(2,1)S(1)}, bf16[48,768]{1,0:T(8,128)(2,1)S(1)}, u32[]{:S(2)}, u32[]{:S(2)}) collective-permute-start(bf16[48,768]{1,0:T(8,128)(2,1)S(1)} %constant_dynamic-slice_fusion.3.refs_3_), channel_id=1, source_target_pairs={{0,1},{1,0},{2,3},{3,2},{4,5},{5,4},{6,7},{7,6},{8,9},{9,8},{10,11... | collective-permute-start | bytes 221192 | tf_op jit(solution)/shard_map/ppermute | solution.py:133
  13.3 2.6 %collective-permute-start.3 = (bf16[48,768]{1,0:T(8,128)(2,1)S(1)}, bf16[48,768]{1,0:T(8,128)(2,1)S(1)}, u32[]{:S(2)}, u32[]{:S(2)}) collective-permute-start(bf16[48,768]{1,0:T(8,128)(2,1)S(1)} %constant_dynamic-slice_fusion.3.refs_3_), channel_id=1, source_target_pairs={{0,2},{1,3},{2,0},{3,1},{4,6},{5,7},{6,4},{7,5},{8,10},{9,11},{10,... | collective-permute-start | bytes 221192 | tf_op jit(solution)/shard_map/ppermute | solution.py:133
  15.9 0.0 collective-permute-start.4
  15.9 1.7 %collective-permute-start.9 = (bf16[96,512]{1,0:T(8,128)(2,1)S(1)}, bf16[96,512]{1,0:T(8,128)(2,1)S(1)}, u32[]{:S(2)}, u32[]{:S(2)}) collective-permute-start(bf16[96,512]{1,0:T(8,128)(2,1)S(1)} %get-tuple-element.16), channel_id=1, source_target_pairs={{0,8},{4,12},{8,0},{12,4},{16,24},{20,28},{24,16},{28,20},{1,9},{5... | collective-permute-start | bytes 294920 | tf_op jit(solution)/shard_map/ppermute | solution.py:133
  17.6 1.1 %shard_map.68 = (bf16[2,512,768]{2,1,0:T(8,128)(2,1)S(1)}, bf16[512,64]{1,0:T(8,128)(2,1)S(1)}) custom-call(bf16[256,768]{1,0:T(8,128)(2,1)S(1)} %copy-done.1, s32[1,256]{1,0:T(1,128)S(1)} %bitcast.22, bf16[256,768]{1,0:T(8,128)(2,1)S(1)} %collective-permute-done.refs_2_, s32[1,256]{1,0:T(1,128)S(1)} %collective-permute-done.1.refs_3_), custom_call_target="tpu_custom_call" | custom-call | tf_op jit(solution)/shard_map/pallas_call | solution.py:118
  18.7 1.4 %collective-permute-done.3.refs_5_ = bf16[48,768]{1,0:T(8,128)(2,1)S(1)} collective-permute-done((bf16[48,768]{1,0:T(8,128)(2,1)S(1)}, bf16[48,768]{1,0:T(8,128)(2,1)S(1)}, u32[]{:S(2)}, u32[]{:S(2)}) %collective-permute-start.3) | collective-permute-done | bytes 73760 | tf_op jit(solution)/shard_map/ppermute | solution.py:133
  20.1 1.9 %collective-permute-done.4.refs_6_ = bf16[48,768]{1,0:T(8,128)(2,1)S(1)} collective-permute-done((bf16[48,768]{1,0:T(8,128)(2,1)S(1)}, bf16[48,768]{1,0:T(8,128)(2,1)S(1)}, u32[]{:S(2)}, u32[]{:S(2)}) %collective-permute-start.4) | collective-permute-done | bytes 73760 | tf_op jit(solution)/shard_map/ppermute | solution.py:133
  22.0 1.6 %shard_map.69 = bf16[8,2,64,256]{3,2,1,0:T(8,128)(2,1)} custom-call(s32[1]{0:T(128)} %bitcast.refs_0_, bf16[2,512,768]{2,1,0:T(8,128)(2,1)S(1)} %get-tuple-element.6.refs_1_, bf16[512,64]{1,0:T(8,128)(2,1)S(1)} %get-tuple-element.7.refs_2_, bf16[48,768]{1,0:T(8,128)(2,1)S(1)} %constant_dynamic-slice_fusion.3.refs_3_, ...), custom_call_target="tpu_custom_call" | custom-call | tf_op jit(solution)/shard_map/pallas_call | solution.py:118
  23.6 3.7 %all-to-all-start = ((bf16[8,128,256]{2,1,0:T(8,128)(2,1)}), bf16[8,128,256]{2,1,0:T(8,128)(2,1)S(1)}, u32[]{:S(2)}, u32[]{:S(2)}) async-start(bf16[8,128,256]{2,1,0:T(8,128)(2,1)} %bitcast.2), calls=%async_computation | async-start | bytes 1048576 | tf_op jit(solution)/shard_map/all_to_all | solution.py:162
  27.3 0.6 %collective-permute-start.10 = (bf16[96,512]{1,0:T(8,128)(2,1)S(1)}, bf16[96,512]{1,0:T(8,128)(2,1)S(1)}, u32[]{:S(2)}, u32[]{:S(2)}) collective-permute-start(bf16[96,512]{1,0:T(8,128)(2,1)S(1)} %broadcast_select_fusion.3.refs_2_), channel_id=1, source_target_pairs={{0,4},{4,0},{8,12},{12,8},{16,20},{20,16},{24,28},{28,24},{1,5},{5... | collective-permute-start | bytes 294920 | tf_op jit(solution)/shard_map/ppermute | solution.py:133
  27.9 0.1 collective-permute-start.11
  28.0 9.0 %all-to-all-done = bf16[8,128,256]{2,1,0:T(8,128)(2,1)S(1)} async-done(((bf16[8,128,256]{2,1,0:T(8,128)(2,1)}), bf16[8,128,256]{2,1,0:T(8,128)(2,1)S(1)}, u32[]{:S(2)}, u32[]{:S(2)}) %all-to-all-start) | async-done | bytes 524320 | tf_op jit(solution)/shard_map/all_to_all | solution.py:162
  37.2 1.9 %shard_map.70 = (f32[512,512]{1,0:T(8,128)}, s32[1,512]{1,0:T(1,128)}) custom-call(bf16[512,256]{1,0:T(8,128)(2,1)S(1)} %bitcast.19, bf16[512,256]{1,0:T(8,128)(2,1)S(1)} %bitcast.20, bf16[96,512]{1,0:T(8,128)(2,1)S(1)} %broadcast_select_fusion.3.refs_2_, bf16[96,512]{1,0:T(8,128)(2,1)S(1)} %broadcast_select_fusion.refs_3_, ...), custom_call_target="tpu_custom_call" | custom-call | tf_op jit(solution)/shard_map/pallas_call | solution.py:118
  (21 shorter events, 0.2 us)
Async XLA Ops:
  0.6 10.8 %copy-start = (bf16[96,768]{1,0:T(8,128)(2,1)S(1)}, bf16[96,768]{1,0:T(8,128)(2,1)}, u32[]{:S(2)}) copy-start(bf16[96,768]{1,0:T(8,128)(2,1)} %param.6) | copy-start | bytes 442372
  0.6 7.3 %copy-start.1 = (bf16[256,768]{1,0:T(8,128)(2,1)S(1)}, bf16[256,768]{1,0:T(8,128)(2,1)}, u32[]{:S(2)}) copy-start(bf16[256,768]{1,0:T(8,128)(2,1)} %refs_0_.1) | copy-start | bytes 1179652
  0.7 7.2 %copy-start.2 = (s32[256]{0:T(256)S(1)}, s32[256]{0:T(256)}, u32[]{:S(2)}) copy-start(s32[256]{0:T(256)} %param.9) | copy-start | bytes 3076
  1.8 1.6 %collective-permute-start.5 = (bf16[192,512]{1,0:T(8,128)(2,1)S(1)}, bf16[192,512]{1,0:T(8,128)(2,1)S(1)}, u32[]{:S(2)}, u32[]{:S(2)}) collective-permute-start(bf16[192,512]{1,0:T(8,128)(2,1)S(1)} %bitcast.25), channel_id=1, source_target_pairs={{0,4},{4,0},{8,12},{12,8},{16,20},{20,16},{24,28},{28,24},{1,5},{5... | collective-permute-start | bytes 589832 | tf_op jit(solution)/shard_map/ppermute | solution.py:133
  3.5 6.0 %collective-permute-start.8 = (bf16[96,512]{1,0:T(8,128)(2,1)S(1)}, bf16[96,512]{1,0:T(8,128)(2,1)S(1)}, u32[]{:S(2)}, u32[]{:S(2)}) collective-permute-start(bf16[96,512]{1,0:T(8,128)(2,1)S(1)} %get-tuple-element.18), channel_id=1, source_target_pairs={{0,16},{4,20},{8,24},{12,28},{16,0},{20,4},{24,8},{28,12},{1,17},{... | collective-permute-start | bytes 294920 | tf_op jit(solution)/shard_map/ppermute | solution.py:133
  6.4 4.6 %collective-permute-start.6 = (bf16[96,512]{1,0:T(8,128)(2,1)S(1)}, bf16[96,512]{1,0:T(8,128)(2,1)S(1)}, u32[]{:S(2)}, u32[]{:S(2)}) collective-permute-start(bf16[96,512]{1,0:T(8,128)(2,1)S(1)} %get-tuple-element.19), channel_id=1, source_target_pairs={{0,8},{4,12},{8,0},{12,4},{16,24},{20,28},{24,16},{28,20},{1,9},{5... | collective-permute-start | bytes 294920 | tf_op jit(solution)/shard_map/ppermute | solution.py:133
  7.9 8.0 %collective-permute-start = (bf16[256,768]{1,0:T(8,128)(2,1)S(1)}, bf16[256,768]{1,0:T(8,128)(2,1)S(1)}, u32[]{:S(2)}, u32[]{:S(2)}) collective-permute-start(bf16[256,768]{1,0:T(8,128)(2,1)S(1)} %copy-done.1), channel_id=1, source_target_pairs={{0,4},{4,0},{8,12},{12,8},{16,20},{20,16},{24,28},{28,24},{1,5},{5... | collective-permute-start | bytes 1179656 | tf_op jit(solution)/shard_map/ppermute | solution.py:133
  7.9 8.0 %collective-permute-start.1 = (s32[1,256]{1,0:T(1,128)S(1)}, s32[1,256]{1,0:T(1,128)S(1)}, u32[]{:S(2)}, u32[]{:S(2)}) collective-permute-start(s32[1,256]{1,0:T(1,128)S(1)} %bitcast.21), channel_id=1, source_target_pairs={{0,4},{4,0},{8,12},{12,8},{16,20},{20,16},{24,28},{28,24},{1,5},{5... | collective-permute-start | bytes 3080 | tf_op jit(solution)/shard_map/ppermute | solution.py:133
  11.1 16.2 %collective-permute-start.7 = (bf16[96,512]{1,0:T(8,128)(2,1)S(1)}, bf16[96,512]{1,0:T(8,128)(2,1)S(1)}, u32[]{:S(2)}, u32[]{:S(2)}) collective-permute-start(bf16[96,512]{1,0:T(8,128)(2,1)S(1)} %get-tuple-element.17), channel_id=1, source_target_pairs={{0,16},{4,20},{8,24},{12,28},{16,0},{20,4},{24,8},{28,12},{1,17},{... | collective-permute-start | bytes 294920 | tf_op jit(solution)/shard_map/ppermute | solution.py:133
  11.4 7.3 %collective-permute-start.2 = (bf16[48,768]{1,0:T(8,128)(2,1)S(1)}, bf16[48,768]{1,0:T(8,128)(2,1)S(1)}, u32[]{:S(2)}, u32[]{:S(2)}) collective-permute-start(bf16[48,768]{1,0:T(8,128)(2,1)S(1)} %constant_dynamic-slice_fusion.3.refs_3_), channel_id=1, source_target_pairs={{0,1},{1,0},{2,3},{3,2},{4,5},{5,4},{6,7},{7,6},{8,9},{9,8},{10,11... | collective-permute-start | bytes 221192 | tf_op jit(solution)/shard_map/ppermute | solution.py:133
  13.3 6.8 %collective-permute-start.3 = (bf16[48,768]{1,0:T(8,128)(2,1)S(1)}, bf16[48,768]{1,0:T(8,128)(2,1)S(1)}, u32[]{:S(2)}, u32[]{:S(2)}) collective-permute-start(bf16[48,768]{1,0:T(8,128)(2,1)S(1)} %constant_dynamic-slice_fusion.3.refs_3_), channel_id=1, source_target_pairs={{0,2},{1,3},{2,0},{3,1},{4,6},{5,7},{6,4},{7,5},{8,10},{9,11},{10,... | collective-permute-start | bytes 221192 | tf_op jit(solution)/shard_map/ppermute | solution.py:133
  15.9 6.2 %collective-permute-start.4 = (bf16[48,768]{1,0:T(8,128)(2,1)S(1)}, bf16[48,768]{1,0:T(8,128)(2,1)S(1)}, u32[]{:S(2)}, u32[]{:S(2)}) collective-permute-start(bf16[48,768]{1,0:T(8,128)(2,1)S(1)} %constant_dynamic-slice_fusion.3.refs_3_), channel_id=1, source_target_pairs={{0,3},{1,2},{2,1},{3,0},{4,7},{5,6},{6,5},{7,4},{8,11},{9,10},{10,... | collective-permute-start | bytes 221192 | tf_op jit(solution)/shard_map/ppermute | solution.py:133
  15.9 12.0 %collective-permute-start.9 = (bf16[96,512]{1,0:T(8,128)(2,1)S(1)}, bf16[96,512]{1,0:T(8,128)(2,1)S(1)}, u32[]{:S(2)}, u32[]{:S(2)}) collective-permute-start(bf16[96,512]{1,0:T(8,128)(2,1)S(1)} %get-tuple-element.16), channel_id=1, source_target_pairs={{0,8},{4,12},{8,0},{12,4},{16,24},{20,28},{24,16},{28,20},{1,9},{5... | collective-permute-start | bytes 294920 | tf_op jit(solution)/shard_map/ppermute | solution.py:133
  23.6 13.5 %all-to-all-start = ((bf16[8,128,256]{2,1,0:T(8,128)(2,1)}), bf16[8,128,256]{2,1,0:T(8,128)(2,1)S(1)}, u32[]{:S(2)}, u32[]{:S(2)}) async-start(bf16[8,128,256]{2,1,0:T(8,128)(2,1)} %bitcast.2), calls=%async_computation | async-start | bytes 1048576 | tf_op jit(solution)/shard_map/all_to_all | solution.py:162
  27.3 9.8 %collective-permute-start.10 = (bf16[96,512]{1,0:T(8,128)(2,1)S(1)}, bf16[96,512]{1,0:T(8,128)(2,1)S(1)}, u32[]{:S(2)}, u32[]{:S(2)}) collective-permute-start(bf16[96,512]{1,0:T(8,128)(2,1)S(1)} %broadcast_select_fusion.3.refs_2_), channel_id=1, source_target_pairs={{0,4},{4,0},{8,12},{12,8},{16,20},{20,16},{24,28},{28,24},{1,5},{5... | collective-permute-start | bytes 294920 | tf_op jit(solution)/shard_map/ppermute | solution.py:133
  27.9 9.2 %collective-permute-start.11 = (bf16[96,512]{1,0:T(8,128)(2,1)S(1)}, bf16[96,512]{1,0:T(8,128)(2,1)S(1)}, u32[]{:S(2)}, u32[]{:S(2)}) collective-permute-start(bf16[96,512]{1,0:T(8,128)(2,1)S(1)} %broadcast_select_fusion.refs_3_), channel_id=1, source_target_pairs={{0,4},{4,0},{8,12},{12,8},{16,20},{20,16},{24,28},{28,24},{1,5},{5... | collective-permute-start | bytes 294920 | tf_op jit(solution)/shard_map/ppermute | solution.py:133
